TPU v7x, 512 devices: a whole 4x4x16 slice. The times are simulated.
512 devices in a mesh: table: 64 (over y, z), replica: 8 (over x, core).
Axes of the slice: x: 4, y: 4, z: 16, core: 2. Of those that a mesh axis runs over, the one named last changes fastest.
Arguments:
- bottom: bfloat16 [131072, 128], P(('table', 'replica')), may hold values from -6 to 6
- hot_ids: int32 [131072, 20], P(('table', 'replica')), may hold values from 0 to 127
- hot_tables: bfloat16 [20, 128, 128], replicated, may hold values from -4 to 4
- cold_owner: int32 [131072, 12], P(('table', 'replica')), may hold values from 0 to 63, all different within a row; in each aligned block of 256 rows (0 to 255, 256 to 511, ...) at most 128 rows name the same one
- cold_row: int32 [131072, 12], P(('table', 'replica')), may hold values from 0 to 255
- cold_rows: float32 [98304, 128], P('table'), may hold values from -3 to 3
- cold_acc: float32 [98304], P('table'), may hold values from 0.001 to 0.1
- u_weight: bfloat16 [3456, 256], P('replica'), may hold values from -0.109375 to 0.109375
- v_weight: float32 [256, 3456], P('replica'), may hold values from -0.375 to 0.375
- v_acc: float32 [256], P('replica'), may hold values from 1 to 100
- cross_bias: float32 [3456], replicated, may hold values from -2 to 2
- head: float32 [3456], replicated, may hold values from -0.109375 to 0.109375
- labels: int32 [131072], P(('table', 'replica')), may hold values 0 or 1
Outputs:
- new_cold_rows: float32 [98304, 128], P('table')
- new_cold_acc: float32 [98304], P('table')
- new_v: float32 [256, 3456], P('replica')
Inputs may be any that keep to these rules, and one draw needn't show every extreme that they name: `cold_owner`: the 12 lookups of one sample name distinct owners; among the samples of one device (aligned blocks of 256 samples) no owner is named more than 128 times, and in every draw some owner is named exactly 128 times in some block.
All inputs are finite; a program needn't handle non-finite values. No bound on the sum of `labels` on one device may be relied on, other than what follows from the above.
Results may differ from a plain program's by a relative error of at most 0.0015.
Values may be sent and summed in bfloat16 or wider, within the bound.
A program may use at most 64 MiB of HBM per device.

v0:
```python
import jax
import jax.numpy as jnp
from jax import lax
from jax.sharding import PartitionSpec as P

NCOLD = 6
LOOK = 2
NHOT = 20


row_rate = 0.1
dense_rate = 0.05
eps_value = 1e-08


def body(
    bottom,
    hot_ids,
    hot_tables,
    cold_owner,
    cold_row,
    cold_rows,
    cold_acc,
    u_weight,
    v_weight,
    v_acc,
    cross_bias,
    head,
    labels,
):
    peers = lax.axis_size("table")
    batch_dev, lookups = cold_owner.shape
    held, embed = cold_rows.shape
    shard_rows = held // NCOLD
    capacity = max(2, min(batch_dev, 8 * batch_dev * lookups // (3 * peers)))
    contract = (((1,), (1,)), ((), ()))
    table_of = jnp.arange(lookups, dtype=jnp.int32) // LOOK
    local_id = (table_of[None, :] * shard_rows + cold_row).reshape(-1)
    owner_flat = cold_owner.reshape(-1)
    hits = (owner_flat[:, None] == jnp.arange(peers, dtype=jnp.int32)[None, :]).astype(jnp.int32)
    place = jnp.sum(jnp.cumsum(hits, axis=0) * hits, axis=1) - 1
    dest = owner_flat * capacity + place
    send_ids = (
        jnp.full((peers * capacity,), held, jnp.int32)
        .at[dest]
        .set(local_id)
        .reshape(peers, capacity)
    )
    served = lax.optimization_barrier(cold_rows.astype(jnp.bfloat16))
    served_pad = jnp.concatenate([served, jnp.zeros((1, embed), jnp.bfloat16)], axis=0)
    asked = lax.all_to_all(send_ids, "table", split_axis=0, concat_axis=0, tiled=True)
    found = served_pad[asked]
    returned = lax.all_to_all(found, "table", split_axis=0, concat_axis=0, tiled=True)
    looked = returned.reshape(peers * capacity, embed)[dest].astype(jnp.float32)
    pooled = jnp.sum(looked.reshape(batch_dev, NCOLD, LOOK, embed), axis=2).astype(jnp.bfloat16)
    hot = hot_tables[jnp.arange(NHOT, dtype=jnp.int32)[None, :], hot_ids]
    first = jnp.concatenate(
        [bottom, pooled.reshape(batch_dev, NCOLD * embed), hot.reshape(batch_dev, NHOT * embed)],
        axis=1,
    )
    u_full, v_half = (
        lax.all_gather(u_weight, "replica", axis=0, tiled=True),
        lax.all_gather(v_weight.astype(jnp.bfloat16), "replica", axis=0, tiled=True),
    )
    low = jnp.dot(first, u_full, preferred_element_type=jnp.float32).astype(jnp.bfloat16)
    mixing = jnp.dot(low, v_half, preferred_element_type=jnp.float32) + cross_bias[None, :]
    wide = first.astype(jnp.float32)
    crossed = wide * mixing + wide
    logit = jnp.dot(crossed, head, precision=lax.Precision.HIGHEST)
    dlogit = jax.nn.sigmoid(logit) - labels.astype(jnp.float32)
    dcross = dlogit[:, None] * head[None, :]
    dmix = (dcross * wide).astype(jnp.bfloat16)
    grad_local = lax.dot_general(
        low, dmix, (((0,), (0,)), ((), ())), preferred_element_type=jnp.float32
    )
    dlow = lax.dot_general(dmix, v_half, contract, preferred_element_type=jnp.float32).astype(
        jnp.bfloat16
    )
    span_end = embed + NCOLD * embed
    dpool = dcross[:, embed:span_end] * (mixing[:, embed:span_end] + 1.0)
    dpool = dpool + lax.dot_general(
        dlow, u_full[embed:span_end], contract, preferred_element_type=jnp.float32
    )
    dpool = dpool.astype(jnp.bfloat16).reshape(batch_dev, NCOLD, 1, embed)
    each = jnp.broadcast_to(dpool, (batch_dev, NCOLD, LOOK, embed)).reshape(
        batch_dev * lookups, embed
    )
    outgoing = (
        jnp.zeros((peers * capacity, embed), jnp.bfloat16)
        .at[dest]
        .set(each)
        .reshape(peers, capacity, embed)
    )
    incoming = lax.all_to_all(outgoing, "table", split_axis=0, concat_axis=0, tiled=True)
    owned = (
        jnp.zeros((held, embed), jnp.float32)
        .at[asked.reshape(-1)]
        .add(incoming.astype(jnp.float32).reshape(peers * capacity, embed), mode="drop")
    )
    grad_rows = lax.psum(owned, "replica")
    new_cold_acc = cold_acc + jnp.mean(grad_rows * grad_rows, axis=1)
    new_cold_rows = cold_rows - row_rate * grad_rows / (jnp.sqrt(new_cold_acc)[:, None] + eps_value)
    rows_here = v_weight.shape[0]
    total = lax.psum(grad_local, ("table", "replica"))
    grad_mine = lax.dynamic_slice_in_dim(total, lax.axis_index("replica") * rows_here, rows_here, 0)
    acc_dense = v_acc + jnp.mean(grad_mine * grad_mine, axis=1)
    new_v = v_weight - dense_rate * grad_mine / (jnp.sqrt(acc_dense)[:, None] + eps_value)
    return (new_cold_rows, new_cold_acc, new_v)


def solution(mesh):
    return jax.shard_map(
        body,
        mesh=mesh,
        in_specs=(
            P(("table", "replica"), None),
            P(("table", "replica"), None),
            P(),
            P(("table", "replica"), None),
            P(("table", "replica"), None),
            P("table", None),
            P("table"),
            P("replica", None),
            P("replica", None),
            P("replica"),
            P(),
            P(),
            P(("table", "replica")),
        ),
        out_specs=(P("table", None), P("table"), P("replica", None)),
        check_vma=False,
    )
```

profile of v0, /device:TPU:8, one launch (start us, length us, event | category | flops | bytes accessed | tf_op | source)
XLA Modules:
  0.0 913.4 jit_solution(10230879108264701170)
XLA Ops:
  7.2 0.8 broadcast_multiply_fusion.1
  8.0 0.8 copy.27
  9.2 0.1 mul.72
  9.4 18.3 %reduce-window.6 = s32[64,24,128]{2,1,0:T(8,128)S(1)} reduce-window(s32[64,24,128]{2,1,0:T(8,128)S(1)} %fusion.14, s32[]{:T(128)} %constant.21.clone.1), window={size=1x1x128 pad=0_0x0_0x127_0}, to_apply=%region_0.1 | reduce-window | flops 24969216 | bytes 1572868 | tf_op jit(solution)/shard_map/reduce-window
  27.7 0.3 slice.26
  28.0 0.4 copy.37
  28.4 0.2 reduce-window.9
  28.6 0.3 broadcast_add_fusion
  28.9 0.2 fusion.12
  29.4 12.4 %scatter_custom_fusion = s32[8192]{0:T(1024)} fusion(s32[3072]{0:T(1024)S(1)} %bitcast.61, s32[3072]{0:T(1024)S(1)} %reshape.213, s32[]{:T(128)} %constant.19.clone.1), kind=kCustom, calls=%fused_computation.47 | custom fusion | bytes 32772 | tf_op jit(solution)/shard_map/scatter | solution.py:46
  41.8 18.7 %all-to-all-start = ((s32[64,1,128]{2,1,0:T(1,128)}), s32[64,1,128]{2,1,0:T(1,128)S(1)}, u32[]{:S(2)}, u32[]{:S(2)}) async-start(s32[64,1,128]{2,1,0:T(1,128)} %bitcast.5), calls=%async_computation | async-start | bytes 65536 | tf_op jit(solution)/shard_map/all_to_all | solution.py:51
  60.6 13.3 %all-to-all-done = s32[64,1,128]{2,1,0:T(1,128)S(1)} async-done(((s32[64,1,128]{2,1,0:T(1,128)}), s32[64,1,128]{2,1,0:T(1,128)S(1)}, u32[]{:S(2)}, u32[]{:S(2)}) %all-to-all-start) | async-done | bytes 32800 | tf_op jit(solution)/shard_map/all_to_all | solution.py:51
  74.0 29.4 %gather_fusion = bf16[8192,128]{1,0:T(8,128)(2,1)} fusion(bf16[1537,128]{1,0:T(8,128)(2,1)S(1)} %concatenate.9, s32[8192]{0:T(1024)S(1)} %fusion.18), kind=kCustom, calls=%fused_computation | custom fusion | bytes 4227072 | tf_op jit(solution)/shard_map/gather | solution.py:52
  103.4 5.7 all-to-all-start.1
  109.2 0.7 all-gather.3.cloned.1.call-update
  110.0 0.7 convert_element_type.52
  110.7 0.6 reshape.240
  111.5 0.1 reshape.203
  111.6 50.6 %gather_fusion.2 = bf16[5120,128]{1,0:T(8,128)(2,1)} fusion(bf16[20,128,128]{2,1,0:T(8,128)(2,1)S(1)} %copy-done, s32[5120]{0:T(1024)S(1)} %reshape.203), kind=kCustom, calls=%fused_computation.2 | custom fusion | bytes 2662400 | tf_op jit(solution)/shard_map/gather | solution.py:56
  162.1 3.8 reshape.180
  165.9 0.6 broadcast_clamp_fusion
  166.5 39.7 %all-to-all-done.1 = bf16[64,128,128]{2,1,0:T(8,128)(2,1)S(1)} async-done(((bf16[64,128,128]{2,1,0:T(8,128)(2,1)}), bf16[64,128,128]{2,1,0:T(8,128)(2,1)S(1)}, u32[]{:S(2)}, u32[]{:S(2)}) %all-to-all-start.1) | async-done | bytes 2097184 | tf_op jit(solution)/shard_map/all_to_all | solution.py:53
  206.3 10.6 %gather_fusion.1 = bf16[3072,128]{1,0:T(8,128)(2,1)S(1)} fusion(bf16[8192,128]{1,0:T(8,128)(2,1)S(1)} %bitcast.49, s32[3072]{0:T(1024)} %broadcast_clamp_fusion), kind=kCustom, calls=%fused_computation.1 | custom fusion | bytes 1585152 | tf_op jit(solution)/shard_map/gather | solution.py:54
  216.9 2.1 reduce
  219.1 0.3 copy.32
  219.4 0.2 copy.34
  219.6 2.5 convolution_convert_fusion.1
  222.2 2.2 convolution_add_fusion
  224.5 1.7 copy-done.1
  226.2 3.0 fusion.3
  229.3 2.1 broadcast_multiply_fusion
  231.4 3.0 fusion.4
  234.4 0.2 copy.35
  234.6 0.3 copy.36
  234.9 0.5 broadcast_in_dim.17
  235.5 10.3 %scatter_custom_fusion.1 = bf16[8192,128]{1,0:T(8,128)(2,1)} fusion(s32[3072]{0:T(1024)} %bitcast.63, bf16[3072,128]{1,0:T(8,128)(2,1)S(1)} %bitcast.57, bf16[]{:T(256)} %constant.26.clone.1), kind=kCustom, calls=%fused_computation.19 | custom fusion | bytes 2097664 | tf_op jit(solution)/shard_map/scatter | solution.py:91
  245.8 7.3 all-to-all-start.2
  253.2 3.9 fusion.7
  257.2 0.7 copy-done.8
  257.9 0.6 compare_select_fusion
  258.5 522.4 %all-reduce.6.cloned.1.call-done = f32[256,3456]{1,0:T(8,128)} async-done(((f32[256,3456]{1,0:T(8,128)}), f32[256,3456]{1,0:T(8,128)}) %all-reduce.6.cloned.1.call-update) | async-done | bytes 3538960 | tf_op jit(solution)/shard_map/psum | solution.py:104
  780.9 1.1 multiply_reduce_fusion.1
  782.1 45.2 %scatter_custom_fusion.2 = f32[1536,128]{1,0:T(8,128)} fusion(s32[8192]{0:T(1024)} %bitcast.65, bf16[8192,128]{1,0:T(8,128)(2,1)S(1)} %bitcast.51, f32[]{:T(128)} %constant.18.clone.1), kind=kCustom, calls=%fused_computation.9 | custom fusion | flops 2097152 | bytes 2884096 | tf_op jit(solution)/shard_map/scatter-add | solution.py:98
  827.3 2.0 divide_subtract_fusion.1
  829.4 73.2 %all-reduce.4.cloned.1.call-done = f32[1536,128]{1,0:T(8,128)} async-done(((f32[1536,128]{1,0:T(8,128)}), f32[1536,128]{1,0:T(8,128)}) %all-reduce.4.cloned.1.call-update) | async-done | bytes 786448 | tf_op jit(solution)/shard_map/psum | solution.py:100
  902.5 1.4 multiply_reduce_fusion
  903.9 0.6 sqrt_add_fusion
  904.6 2.3 divide_subtract_fusion
  (73 shorter events, 1.4 us)
Async XLA Ops:
  7.2 104.4 %copy-start = (bf16[20,128,128]{2,1,0:T(8,128)(2,1)S(1)}, bf16[20,128,128]{2,1,0:T(8,128)(2,1)}, u32[]{:S(2)}) copy-start(bf16[20,128,128]{2,1,0:T(8,128)(2,1)} %param.15) | copy-start | bytes 1966084
  9.4 19.7 %copy-start.15 = (s32[256,12]{0,1:T(8,128)S(1)}, s32[256,12]{0,1:T(8,128)}, u32[]{:S(2)}) copy-start(s32[256,12]{0,1:T(8,128)} %param.17) | copy-start | bytes 36868
  9.4 51.2 %copy-start.2 = (f32[1536,128]{1,0:T(8,128)S(1)}, f32[1536,128]{1,0:T(8,128)}, u32[]{:S(2)}) copy-start(f32[1536,128]{1,0:T(8,128)} %param.18) | copy-start | bytes 2359300
  29.4 136.5 %copy-start.13 = (s32[3072,1]{0,1:T(1,128)}, s32[3072,1]{0,1:T(1,128)S(1)}, u32[]{:S(2)}) copy-start(s32[3072,1]{0,1:T(1,128)S(1)} %compare_select_fusion.2) | copy-start | bytes 36868
  41.8 32.2 %all-to-all-start = ((s32[64,1,128]{2,1,0:T(1,128)}), s32[64,1,128]{2,1,0:T(1,128)S(1)}, u32[]{:S(2)}, u32[]{:S(2)}) async-start(s32[64,1,128]{2,1,0:T(1,128)} %bitcast.5), calls=%async_computation | async-start | bytes 65536 | tf_op jit(solution)/shard_map/all_to_all | solution.py:51
  74.0 29.4 %copy-start.7 = (s32[64,1,128]{2,1,0:T(1,128)}, s32[64,1,128]{2,1,0:T(1,128)S(1)}, u32[]{:S(2)}) copy-start(s32[64,1,128]{2,1,0:T(1,128)S(1)} %all-to-all-done) | copy-start | bytes 98308
  103.4 6.5 copy-start.4
  103.4 7.3 copy-start.12
  103.4 7.9 copy-start.14
  103.4 102.8 %all-to-all-start.1 = ((bf16[64,128,128]{2,1,0:T(8,128)(2,1)}), bf16[64,128,128]{2,1,0:T(8,128)(2,1)S(1)}, u32[]{:S(2)}, u32[]{:S(2)}) async-start(bf16[64,128,128]{2,1,0:T(8,128)(2,1)} %bitcast.50), calls=%async_computation.1 | async-start | bytes 4194304 | tf_op jit(solution)/shard_map/all_to_all | solution.py:53
  109.2 110.4 %all-gather.3.cloned.1.call-start = ((), (), s32[]{:S(2)}) async-start(), calls=%async_computation.3 | async-start | bytes 1990656 | tf_op jit(solution)/shard_map/all_gather | solution.py:62
  109.9 112.3 %all-gather.5.cloned.1.call-start = ((), (), s32[]{:S(2)}) async-start(), calls=%async_computation.4 | async-start | bytes 1990656 | tf_op jit(solution)/shard_map/all_gather | solution.py:63
  219.5 2.7 copy-start.11
  222.1 2.3 copy-start.9
  222.1 4.1 copy-start.6
  222.2 4.1 copy-start.16
  222.2 4.0 copy-start.21
  224.5 1.8 copy-start.1
  226.2 3.1 copy-start.20
  229.3 2.1 copy-start.5
  229.3 5.1 copy-start.18
  235.4 17.7 %copy-start.10 = (bf16[256,256]{1,0:T(8,128)(2,1)S(1)}, bf16[256,256]{1,0:T(8,128)(2,1)}, u32[]{:S(2)}) copy-start(bf16[256,256]{1,0:T(8,128)(2,1)} %copy-done.9) | copy-start | bytes 393220
  235.5 17.7 %copy-start.19 = (f32[256]{0:T(256)S(1)}, f32[256]{0:T(256)}, u32[]{:S(2)}) copy-start(f32[256]{0:T(256)} %copy-done.18) | copy-start | bytes 3076
  235.5 17.7 %copy-start.22 = (bf16[256,128]{1,0:T(8,128)(2,1)S(1)}, bf16[256,128]{1,0:T(8,128)(2,1)}, u32[]{:S(2)}) copy-start(bf16[256,128]{1,0:T(8,128)(2,1)} %param.13) | copy-start | bytes 196612
  245.8 536.3 %all-to-all-start.2 = ((bf16[64,128,128]{2,1,0:T(8,128)(2,1)}), bf16[64,128,128]{2,1,0:T(8,128)(2,1)S(1)}, u32[]{:S(2)}, u32[]{:S(2)}) async-start(bf16[64,128,128]{2,1,0:T(8,128)(2,1)} %bitcast.52), calls=%async_computation.2 | async-start | bytes 4194304 | tf_op jit(solution)/shard_map/all_to_all | solution.py:94
  253.1 527.8 %all-reduce.6.cloned.1.call-start = ((), (), s32[]{:S(2)}) async-start(), calls=%async_computation.6 | async-start | bytes 7077888 | tf_op jit(solution)/shard_map/psum | solution.py:104
  257.1 0.8 copy-start.8
  257.1 525.0 %copy-start.23 = (f32[32]{0:T(128)S(1)}, f32[32]{0:T(128)}, u32[]{:S(2)}) copy-start(f32[32]{0:T(128)} %param.22) | copy-start | bytes 388
  257.1 646.8 %copy-start.17 = (f32[1536]{0:T(1024)S(1)}, f32[1536]{0:T(1024)}, u32[]{:S(2)}) copy-start(f32[1536]{0:T(1024)} %param.19) | copy-start | bytes 18436
  257.1 645.4 %all-reduce.4.cloned.1.call-start = ((), (), s32[]{:S(2)}) async-start(), calls=%async_computation.5 | async-start | bytes 1572864 | tf_op jit(solution)/shard_map/psum | solution.py:100
  258.5 646.1 %copy-start.3 = (f32[1536,128]{1,0:T(8,128)S(1)}, f32[1536,128]{1,0:T(8,128)}, u32[]{:S(2)}) copy-start(f32[1536,128]{1,0:T(8,128)} %param.18) | copy-start | bytes 2359300
Sparse Core Ops, SparseCore 0:
  112.1 33.2 all-gather.2
  148.1 32.7 all-gather.4
  259.4 521.5 all-reduce.5
  827.5 75.0 all-reduce.3
where the time goes:
time: 914 us; the launch traced here: 913 us
  waiting for transfers between devices  649 us (71%)
  local copies, waits for them, and re-layouts  124 us (14%)
  other arithmetic  78.9 us (9%)
  starting transfers between devices  32 us (4%)
  matrix products  14.6 us (2%)
  between operations  14.2 us (2%)
    psum x1, waiting for transfers between devices, body(): total = lax.psum(grad_local, ('table', 'replica'))  522 us
    psum x1, waiting for transfers between devices, body(): grad_rows = lax.psum(owned, 'replica')  73.2 us
    gather x1, local copies, waits for them, and re-layouts, body(): hot = hot_tables[jnp.arange(NHOT, dtype=jnp.int32)[None, :], hot_ids]  50.6 us
    scatter-add x1, other arithmetic, body(): owned = jnp.zeros((held, embed), jnp.float32).at[asked.reshape(-1)].add(i...  45.2 us
    all_to_all x1, waiting for transfers between devices, body(): lax.all_to_all(found, 'table', split_axis=0, concat_axis=0, tiled=True)  39.7 us
    gather x1, local copies, waits for them, and re-layouts, body(): found = served_pad[asked]  29.4 us
    another operation x3, other arithmetic  18.8 us
    all_to_all x1, starting transfers between devices, body(): lax.all_to_all(send_ids, 'table', split_axis=0, concat_axis=0, tiled=True)  18.7 us
  transfers between devices with their start and end apart: 7, of which 4 were waited for; matrix products, arithmetic and copies ran while one was open for 9% of the time, Pallas kernels for 0%

commit v1 on v0

v1 whole, which is shorter than its diff:
```python
import functools
import jax
import jax.numpy as jnp
from jax import lax
from jax.experimental import pallas as pl
from jax.experimental.pallas import tpu as pltpu
from jax.sharding import PartitionSpec as P

NCOLD = 6
LOOK = 2
NHOT = 20
LOOKUPS = NCOLD * LOOK
E = 128
B = 256
ROWS = 256
SLOTS = 128
GROUP = 64
WIDE = NCOLD * E
PART = WIDE // 8
CROSS = 3456
PADDED = 3584
VCHUNKS = 14
VCOLS = 256
MESH = pl.DeviceIdType.MESH

row_rate = 0.1
dense_rate = 0.05
eps_value = 1e-08

f32 = jnp.float32
bf16 = jnp.bfloat16
i32 = jnp.int32
NT = (((1,), (1,)), ((), ()))


def place_of():
    table, rep = lax.axis_index("table"), lax.axis_index("replica")
    return table // 16, table % 16, rep


def dev(y, z, rep):
    return {"table": y * 16 + z, "replica": rep}


def member_of(y, z, rep):
    return y * 16 + rep * 2 + z % 2


def member_dev(member, z):
    return dev(member // 16, z - z % 2 + member % 2, (member // 2) % 8)


def peer(i, y, z, rep):
    py = (y + i // 16) % 4
    px = (rep // 2 + (i // 4) % 4) % 4
    pc = (rep + (i // 2) % 2) % 2
    pz = (z + i) % 2
    return py * 16 + px * 4 + pc * 2 + pz


def peer_back(i, y, z, rep):
    py = (y + 4 - i // 16) % 4
    px = (rep // 2 + 4 - (i // 4) % 4) % 4
    pc = (rep + (i // 2) % 2) % 2
    pz = (z + i) % 2
    return py * 16 + px * 4 + pc * 2 + pz


def greet(y, z, rep):
    bar = pltpu.get_barrier_semaphore()

    def group(i, carry):
        pl.semaphore_signal(
            bar, inc=1, device_id=member_dev(peer(i, y, z, rep), z), device_id_type=MESH
        )
        return carry

    lax.fori_loop(1, GROUP, group, 0)
    return bar


def tables(owner_ref, row_ref, pos, tab, rows):
    owners = lax.broadcasted_iota(i32, (GROUP, B), 0)
    named = jnp.zeros((GROUP, B), f32)
    table = jnp.zeros((GROUP, B), f32)
    row = jnp.zeros((GROUP, B), f32)
    for k in range(LOOKUPS):
        hit = owners == owner_ref[k : k + 1, :]
        named = jnp.where(hit, 1.0, named)
        table = jnp.where(hit, float(k // LOOK), table)
        if rows is not None:
            row = jnp.where(hit, row_ref[k : k + 1, :].astype(f32), row)
    before = jnp.where(
        lax.broadcasted_iota(i32, (B, B), 0) < lax.broadcasted_iota(i32, (B, B), 1), 1.0, 0.0
    ).astype(bf16)
    place = jnp.dot(named.astype(bf16), before, preferred_element_type=f32)
    pos[...] = jnp.where(named > 0.0, place, -1.0)
    tab[...] = table
    if rows is not None:
        rows[...] = row


def slots_of(pos, o):
    lines = lax.broadcasted_iota(i32, (SLOTS, B), 0).astype(f32)
    return jnp.where(lines == pos[pl.ds(o, 1), :], 1.0, 0.0).astype(bf16)


def rows_of(code):
    lines = lax.broadcasted_iota(i32, (ROWS, code.shape[1]), 0)
    return jnp.where(lines == code % ROWS, 1.0, 0.0).astype(bf16)


def forward_kernel(
    owner_ref, row_ref, part_ref, pooled_ref, asked_ref,
    held, replies, back, ask, pos, tab, rows, picks, pooled,
    held_send, held_recv, ask_send, ask_recv, rep_send, rep_recv, own_sem,
):
    y, z, rep = place_of()
    me = member_of(y, z, rep)
    bar = greet(y, z, rep)
    home = z // 2

    def holder(j):
        return (z + 2 * j) % 16

    def source(j):
        return rep * 2 + z % 2, (rep + j) % 8

    def greet_source(j, n):
        sz, srep = source(j)
        other = jnp.logical_or(sz != z, srep != rep)

        @pl.when(other)
        def _():
            pl.semaphore_signal(bar, inc=1, device_id=dev(y, sz, srep), device_id_type=MESH)

        return n

    lax.fori_loop(0, 8, greet_source, 0)
    self_holder = home == rep
    pl.semaphore_wait(bar, GROUP - 1 + 8 - jnp.where(self_holder, 1, 0).astype(i32))

    def part_copy(j):
        return pltpu.make_async_remote_copy(
            src_ref=part_ref,
            dst_ref=held.at[rep],
            send_sem=held_send.at[j],
            recv_sem=held_recv.at[rep],
            device_id=dev(y, holder(j), home),
            device_id_type=MESH,
        )

    def send_part(j, carry):
        other = jnp.logical_or(holder(j) != z, home != rep)

        @pl.when(other)
        def _():
            part_copy(j).start()

        return carry

    lax.fori_loop(0, 8, send_part, 0)
    own = pltpu.make_async_copy(part_ref, held.at[rep], own_sem)

    @pl.when(self_holder)
    def _():
        own.start()

    tables(owner_ref, row_ref, pos, tab, rows)
    lines16 = lax.broadcasted_iota(i32, (16, B), 0)

    def ask_copy(m):
        return pltpu.make_async_remote_copy(
            src_ref=ask.at[m],
            dst_ref=asked_ref.at[me],
            send_sem=ask_send.at[m],
            recv_sem=ask_recv.at[me],
            device_id=member_dev(m, z),
            device_id_type=MESH,
        )

    def ask_pair(p, carry):
        a, b = peer(2 * p, y, z, rep), peer(2 * p + 1, y, z, rep)
        pick_a, pick_b = slots_of(pos, a), slots_of(pos, b)
        picks[a] = pick_a
        picks[b] = pick_b
        lhs = jnp.where(lines16 == 0, rows[pl.ds(a, 1), :], 0.0)
        lhs = jnp.where(lines16 == 1, tab[pl.ds(a, 1), :], lhs)
        lhs = jnp.where(lines16 == 2, rows[pl.ds(b, 1), :], lhs)
        lhs = jnp.where(lines16 == 3, tab[pl.ds(b, 1), :], lhs).astype(bf16)
        got = lax.dot_general(
            lhs, jnp.concatenate([pick_a, pick_b], axis=0), NT, preferred_element_type=f32
        )
        code_a = (got[0:1, :SLOTS] + got[1:2, :SLOTS] * float(ROWS)).astype(i32)
        code_b = (got[2:3, SLOTS:] + got[3:4, SLOTS:] * float(ROWS)).astype(i32)
        ask[a] = jnp.broadcast_to(code_a, (8, SLOTS))
        ask[b] = jnp.broadcast_to(code_b, (8, SLOTS))

        @pl.when(p > 0)
        def _():
            ask_copy(a).start()

        @pl.when(p == 0)
        def _():
            asked_ref[me] = ask[me]

        ask_copy(b).start()
        return carry

    lax.fori_loop(0, GROUP // 2, ask_pair, 0)

    def await_part(j, carry):
        sz, srep = source(j)
        other = jnp.logical_or(sz != z, srep != rep)

        @pl.when(other)
        def _():
            pltpu.make_async_remote_copy(
                src_ref=part_ref,
                dst_ref=held.at[srep],
                send_sem=held_send.at[0],
                recv_sem=held_recv.at[srep],
                device_id=dev(y, sz, srep),
                device_id_type=MESH,
            ).wait_recv()

        return carry

    lax.fori_loop(0, 8, await_part, 0)

    @pl.when(self_holder)
    def _():
        own.wait()

    def reply_copy(m):
        return pltpu.make_async_remote_copy(
            src_ref=back.at[m],
            dst_ref=replies.at[me],
            send_sem=rep_send.at[m],
            recv_sem=rep_recv.at[me],
            device_id=member_dev(m, z),
            device_id_type=MESH,
        )

    def await_ask(m):
        pltpu.make_async_remote_copy(
            src_ref=ask.at[m],
            dst_ref=asked_ref.at[m],
            send_sem=ask_send.at[m],
            recv_sem=ask_recv.at[m],
            device_id=member_dev(m, z),
            device_id_type=MESH,
        ).wait_recv()

    def reply_pair(p, carry):
        a, b = peer_back(2 * p, y, z, rep), peer_back(2 * p + 1, y, z, rep)

        @pl.when(p > 0)
        def _():
            await_ask(a)

        await_ask(b)
        code = jnp.concatenate([asked_ref[a][0:1, :], asked_ref[b][0:1, :]], axis=1)
        table = code // ROWS
        found = jnp.dot(
            held[...].reshape(WIDE, ROWS), rows_of(code), preferred_element_type=f32
        )
        out = found[0:E]
        for t in range(1, NCOLD):
            out = jnp.where(table == t, found[t * E : (t + 1) * E], out)
        out = out.astype(bf16)
        back[a] = out[:, :SLOTS]
        back[b] = out[:, SLOTS:]

        @pl.when(p > 0)
        def _():
            reply_copy(a).start()

        @pl.when(p == 0)
        def _():
            replies[me] = back[me]

        reply_copy(b).start()
        return carry

    lax.fori_loop(0, GROUP // 2, reply_pair, 0)

    pooled[...] = jnp.zeros((WIDE, B), f32)

    def await_reply(m):
        pltpu.make_async_remote_copy(
            src_ref=back.at[m],
            dst_ref=replies.at[m],
            send_sem=rep_send.at[m],
            recv_sem=rep_recv.at[m],
            device_id=member_dev(m, z),
            device_id_type=MESH,
        ).wait_recv()

    def pool_pair(p, carry):
        a, b = peer(2 * p, y, z, rep), peer(2 * p + 1, y, z, rep)

        @pl.when(p > 0)
        def _():
            await_reply(a)

        await_reply(b)
        got_a = jnp.dot(replies[a], picks[a], preferred_element_type=f32)
        got_b = jnp.dot(replies[b], picks[b], preferred_element_type=f32)
        tab_a, tab_b = tab[pl.ds(a, 1), :], tab[pl.ds(b, 1), :]
        for t in range(NCOLD):
            more = jnp.where(tab_a == float(t), got_a, 0.0) + jnp.where(tab_b == float(t), got_b, 0.0)
            pooled[t * E : (t + 1) * E, :] += more
        return carry

    lax.fori_loop(0, GROUP // 2, pool_pair, 0)
    pooled_ref[...] = pooled[...].astype(bf16)

    def drain(i, carry):
        m = peer(i, y, z, rep)
        ask_copy(m).wait_send()
        reply_copy(m).wait_send()
        return carry

    lax.fori_loop(1, GROUP, drain, 0)

    def drain_part(j, carry):
        other = jnp.logical_or(holder(j) != z, home != rep)

        @pl.when(other)
        def _():
            part_copy(j).wait_send()

        return carry

    lax.fori_loop(0, 8, drain_part, 0)


def backward_kernel(
    owner_ref, dpool_ref, asked_ref, grad_ref,
    arrived, out, pos, tab, acc, part_out, part_in, whole,
    out_send, out_recv, part_send, part_recv, all_send, all_recv,
):
    y, z, rep = place_of()
    me = member_of(y, z, rep)
    bar = greet(y, z, rep)
    home = z // 2
    owner_z = rep * 2 + z % 2
    self_holder = home == rep

    def source(j):
        return (z + 2 * j) % 16, home

    def greet_source(j, n):
        sz, srep = source(j)
        other = jnp.logical_or(sz != z, srep != rep)

        @pl.when(other)
        def _():
            pl.semaphore_signal(bar, inc=1, device_id=dev(y, sz, srep), device_id_type=MESH)

        return n

    lax.fori_loop(0, 8, greet_source, 0)
    pl.semaphore_wait(bar, GROUP - 1 + 8 - jnp.where(self_holder, 1, 0).astype(i32))
    tables(owner_ref, None, pos, tab, None)

    def out_copy(m):
        return pltpu.make_async_remote_copy(
            src_ref=out.at[m],
            dst_ref=arrived.at[me],
            send_sem=out_send.at[m],
            recv_sem=out_recv.at[me],
            device_id=member_dev(m, z),
            device_id_type=MESH,
        )

    def pack(m):
        which = tab[pl.ds(m, 1), :]
        grads = dpool_ref[0:E, :]
        for t in range(1, NCOLD):
            grads = jnp.where(which == float(t), dpool_ref[t * E : (t + 1) * E, :], grads)
        out[m] = lax.dot_general(
            grads.astype(bf16), slots_of(pos, m), NT, preferred_element_type=f32
        ).astype(bf16)

    def pack_pair(p, carry):
        a, b = peer(2 * p, y, z, rep), peer(2 * p + 1, y, z, rep)
        pack(a)
        pack(b)

        @pl.when(p > 0)
        def _():
            out_copy(a).start()

        @pl.when(p == 0)
        def _():
            arrived[me] = out[me]

        out_copy(b).start()
        return carry

    lax.fori_loop(0, GROUP // 2, pack_pair, 0)
    acc[...] = jnp.zeros((WIDE, ROWS), f32)

    def await_out(m):
        pltpu.make_async_remote_copy(
            src_ref=out.at[m],
            dst_ref=arrived.at[m],
            send_sem=out_send.at[m],
            recv_sem=out_recv.at[m],
            device_id=member_dev(m, z),
            device_id_type=MESH,
        ).wait_recv()

    def add_pair(p, carry):
        a, b = peer_back(2 * p, y, z, rep), peer_back(2 * p + 1, y, z, rep)

        @pl.when(p > 0)
        def _():
            await_out(a)

        await_out(b)
        code = jnp.concatenate([asked_ref[a][0:1, :], asked_ref[b][0:1, :]], axis=1)
        table = code // ROWS
        grads = jnp.concatenate([arrived[a], arrived[b]], axis=1).astype(f32)
        lhs = jnp.concatenate(
            [jnp.where(table == t, grads, 0.0).astype(bf16) for t in range(NCOLD)], axis=0
        )
        acc[...] += lax.dot_general(lhs, rows_of(code), NT, preferred_element_type=f32)
        return carry

    lax.fori_loop(0, GROUP // 2, add_pair, 0)

    def part_copy(j):
        return pltpu.make_async_remote_copy(
            src_ref=part_out.at[j],
            dst_ref=part_in.at[home],
            send_sem=part_send.at[j],
            recv_sem=part_recv.at[home],
            device_id=dev(y, owner_z, j),
            device_id_type=MESH,
        )

    def send_part(j, carry):
        part_out[j] = acc[pl.ds(pl.multiple_of(j * PART, PART), PART), :].astype(bf16)
        other = jnp.logical_or(owner_z != z, j != rep)

        @pl.when(other)
        def _():
            part_copy(j).start()

        @pl.when(jnp.logical_not(other))
        def _():
            part_in[home] = part_out[j]

        return carry

    lax.fori_loop(0, 8, send_part, 0)

    def await_part(j, carry):
        sz, srep = source(j)
        other = jnp.logical_or(sz != z, srep != rep)

        @pl.when(other)
        def _():
            pltpu.make_async_remote_copy(
                src_ref=part_out.at[0],
                dst_ref=part_in.at[sz // 2],
                send_sem=part_send.at[0],
                recv_sem=part_recv.at[sz // 2],
                device_id=dev(y, sz, srep),
                device_id_type=MESH,
            ).wait_recv()

        return carry

    lax.fori_loop(0, 8, await_part, 0)
    total = part_in[0].astype(f32)
    for g in range(1, 8):
        total = total + part_in[g].astype(f32)
    whole[rep] = total.astype(bf16)

    def all_copy(j):
        return pltpu.make_async_remote_copy(
            src_ref=whole.at[rep],
            dst_ref=whole.at[rep],
            send_sem=all_send.at[j],
            recv_sem=all_recv.at[rep],
            device_id=dev(y, z, (rep + j) % 8),
            device_id_type=MESH,
        )

    def send_all(j, carry):
        all_copy(j).start()
        return carry

    lax.fori_loop(1, 8, send_all, 0)

    def await_all(j, carry):
        other = (rep + 8 - j) % 8
        pltpu.make_async_remote_copy(
            src_ref=whole.at[other],
            dst_ref=whole.at[other],
            send_sem=all_send.at[j],
            recv_sem=all_recv.at[other],
            device_id=dev(y, z, other),
            device_id_type=MESH,
        ).wait_recv()
        return carry

    lax.fori_loop(1, 8, await_all, 0)
    grad_ref[...] = whole[...].astype(f32)

    def drain(i, carry):
        out_copy(peer(i, y, z, rep)).wait_send()
        return carry

    lax.fori_loop(1, GROUP, drain, 0)

    def drain_part(j, carry):
        other = jnp.logical_or(owner_z != z, j != rep)

        @pl.when(other)
        def _():
            part_copy(j).wait_send()

        return carry

    lax.fori_loop(0, 8, drain_part, 0)

    def drain_all(j, carry):
        all_copy(j).wait_send()
        return carry

    lax.fori_loop(1, 8, drain_all, 0)


def dense_kernel(
    grad_ref, total_ref,
    core_in, pair, x_in, mine, y_in, column, z_in, strip,
    core_send, core_recv, x_send, x_recv, y_send, y_recv, z_send, z_recv, zb_send, zb_recv, yb_send, yb_recv,
):
    y, z, rep = place_of()
    x, c = rep // 2, rep % 2
    other_c = 1 - c
    bar = pltpu.get_barrier_semaphore()

    def signal(y_, z_, rep_):
        pl.semaphore_signal(bar, inc=1, device_id=dev(y_, z_, rep_), device_id_type=MESH)

    signal(y, z, x * 2 + other_c)
    for k in range(1, 4):
        signal(y, z, ((x + k) % 4) * 2 + c)
        signal((y + k) % 4, z, rep)
    for k in range(1, 16):
        signal(y, (z + k) % 16, rep)
    pl.semaphore_wait(bar, 1 + 3 + 3 + 15)

    core_copies = []
    for k in range(4):
        copy = pltpu.make_async_remote_copy(
            src_ref=grad_ref.at[2 * k + other_c],
            dst_ref=core_in.at[k],
            send_sem=core_send.at[k],
            recv_sem=core_recv.at[k],
            device_id=dev(y, z, x * 2 + other_c),
            device_id_type=MESH,
        )
        copy.start()
        core_copies.append(copy)
    for k in range(4):
        core_copies[k].wait_recv()
    for k in range(4):
        pair[k] = (grad_ref[2 * k + c].astype(f32) + core_in[k].astype(f32)).astype(bf16)

    x_copies = []
    for k in (2, 1, 3):
        to = (x + k) % 4
        copy = pltpu.make_async_remote_copy(
            src_ref=pair.at[to],
            dst_ref=x_in.at[k],
            send_sem=x_send.at[k],
            recv_sem=x_recv.at[k],
            device_id=dev(y, z, to * 2 + c),
            device_id_type=MESH,
        )
        copy.start()
        x_copies.append(copy)
    for copy in x_copies:
        copy.wait_recv()
    mine[...] = (
        pair[x].astype(f32) + x_in[1].astype(f32) + x_in[2].astype(f32) + x_in[3].astype(f32)
    )

    y_copies = []
    for k in (2, 1, 3):
        to = (y + k) % 4
        copy = pltpu.make_async_remote_copy(
            src_ref=mine.at[pl.ds(pl.multiple_of(to * 8, 8), 8), :],
            dst_ref=y_in.at[k],
            send_sem=y_send.at[k],
            recv_sem=y_recv.at[k],
            device_id=dev(to, z, rep),
            device_id_type=MESH,
        )
        copy.start()
        y_copies.append(copy)
    for copy in y_copies:
        copy.wait_recv()
    column[:, CROSS:] = jnp.zeros((8, PADDED - CROSS), f32)
    column[:, :CROSS] = (
        mine[pl.ds(pl.multiple_of(y * 8, 8), 8), :] + y_in[1] + y_in[2] + y_in[3]
    )

    def cols(j):
        return pl.ds(pl.multiple_of(j * VCOLS, VCOLS), VCOLS)

    def z_copy(k):
        to = (z + k) % 16
        return pltpu.make_async_remote_copy(
            src_ref=column.at[:, cols(to)],
            dst_ref=z_in.at[k],
            send_sem=z_send.at[k],
            recv_sem=z_recv.at[k],
            device_id=dev(y, to, rep),
            device_id_type=MESH,
        )

    def z_start(k, carry):
        @pl.when((z + k) % 16 < VCHUNKS)
        def _():
            z_copy(k).start()

        return carry

    lax.fori_loop(1, 16, z_start, 0)

    def zb_copy(k):
        return pltpu.make_async_remote_copy(
            src_ref=strip.at[:, cols(z)],
            dst_ref=strip.at[:, cols(z)],
            send_sem=zb_send.at[k],
            recv_sem=zb_recv.at[z],
            device_id=dev(y, (z + k) % 16, rep),
            device_id_type=MESH,
        )

    @pl.when(z < VCHUNKS)
    def _():
        def z_wait(k, carry):
            pltpu.make_async_remote_copy(
                src_ref=z_in.at[k],
                dst_ref=z_in.at[k],
                send_sem=z_send.at[k],
                recv_sem=z_recv.at[k],
                device_id=dev(y, (z + 16 - k) % 16, rep),
                device_id_type=MESH,
            ).wait_recv()
            return carry

        lax.fori_loop(1, 16, z_wait, 0)
        z_in[0] = column[:, cols(z)]
        total = z_in[0]
        for k in range(1, 16):
            total = total + z_in[k]
        strip[:, cols(z)] = total

        def zb_start(k, carry):
            zb_copy(k).start()
            return carry

        lax.fori_loop(1, 16, zb_start, 0)

    def zb_wait(k, carry):
        other = (z + 16 - k) % 16

        @pl.when(other < VCHUNKS)
        def _():
            pltpu.make_async_remote_copy(
                src_ref=strip.at[:, cols(other)],
                dst_ref=strip.at[:, cols(other)],
                send_sem=zb_send.at[k],
                recv_sem=zb_recv.at[other],
                device_id=dev(y, other, rep),
                device_id_type=MESH,
            ).wait_recv()

        return carry

    lax.fori_loop(1, 16, zb_wait, 0)

    def band(j):
        return pl.ds(pl.multiple_of(j * 8, 8), 8)

    total_ref[band(y), :] = strip[:, :CROSS]
    yb_copies = []
    for k in (2, 1, 3):
        copy = pltpu.make_async_remote_copy(
            src_ref=total_ref.at[band(y), :],
            dst_ref=total_ref.at[band(y), :],
            send_sem=yb_send.at[k],
            recv_sem=yb_recv.at[k],
            device_id=dev((y + k) % 4, z, rep),
            device_id_type=MESH,
        )
        copy.start()
        yb_copies.append(copy)
    for k in (2, 1, 3):
        came = band((y + 4 - k) % 4)
        pltpu.make_async_remote_copy(
            src_ref=total_ref.at[came, :],
            dst_ref=total_ref.at[came, :],
            send_sem=yb_send.at[k],
            recv_sem=yb_recv.at[k],
            device_id=dev((y + 4 - k) % 4, z, rep),
            device_id_type=MESH,
        ).wait_recv()
    for copy in core_copies + x_copies + y_copies + yb_copies:
        copy.wait_send()

    def z_drain(k, carry):
        @pl.when((z + k) % 16 < VCHUNKS)
        def _():
            z_copy(k).wait_send()

        @pl.when(z < VCHUNKS)
        def _():
            zb_copy(k).wait_send()

        return carry

    lax.fori_loop(1, 16, z_drain, 0)


def vmem():
    return pl.BlockSpec(memory_space=pltpu.VMEM)


def dma(n):
    return pltpu.SemaphoreType.DMA((n,))


def forward_call(owner, row, part):
    return pl.pallas_call(
        forward_kernel,
        out_shape=(
            jax.ShapeDtypeStruct((WIDE, B), bf16),
            jax.ShapeDtypeStruct((GROUP, 8, SLOTS), i32),
        ),
        in_specs=[vmem()] * 3,
        out_specs=(vmem(), vmem()),
        scratch_shapes=[
            pltpu.VMEM((8, PART, ROWS), bf16),
            pltpu.VMEM((GROUP, E, SLOTS), bf16),
            pltpu.VMEM((GROUP, E, SLOTS), bf16),
            pltpu.VMEM((GROUP, 8, SLOTS), i32),
            pltpu.VMEM((GROUP, B), f32),
            pltpu.VMEM((GROUP, B), f32),
            pltpu.VMEM((GROUP, B), f32),
            pltpu.VMEM((GROUP, SLOTS, B), bf16),
            pltpu.VMEM((WIDE, B), f32),
            dma(8), dma(8), dma(GROUP), dma(GROUP), dma(GROUP), dma(GROUP),
            pltpu.SemaphoreType.DMA,
        ],
        compiler_params=pltpu.CompilerParams(
            collective_id=0, has_side_effects=True, vmem_limit_bytes=40 << 20
        ),
    )(owner, row, part)


def backward_call(owner, dpool, asked):
    return pl.pallas_call(
        backward_kernel,
        out_shape=jax.ShapeDtypeStruct((8, PART, ROWS), f32),
        in_specs=[vmem()] * 3,
        out_specs=vmem(),
        scratch_shapes=[
            pltpu.VMEM((GROUP, E, SLOTS), bf16),
            pltpu.VMEM((GROUP, E, SLOTS), bf16),
            pltpu.VMEM((GROUP, B), f32),
            pltpu.VMEM((GROUP, B), f32),
            pltpu.VMEM((WIDE, ROWS), f32),
            pltpu.VMEM((8, PART, ROWS), bf16),
            pltpu.VMEM((8, PART, ROWS), bf16),
            pltpu.VMEM((8, PART, ROWS), bf16),
            dma(GROUP), dma(GROUP), dma(8), dma(8), dma(8), dma(8),
        ],
        compiler_params=pltpu.CompilerParams(
            collective_id=1, has_side_effects=True, vmem_limit_bytes=40 << 20
        ),
    )(owner, dpool, asked)


def dense_call(grad):
    return pl.pallas_call(
        dense_kernel,
        out_shape=jax.ShapeDtypeStruct((32, CROSS), f32),
        in_specs=[vmem()],
        out_specs=vmem(),
        scratch_shapes=[
            pltpu.VMEM((4, 32, CROSS), bf16),
            pltpu.VMEM((4, 32, CROSS), bf16),
            pltpu.VMEM((4, 32, CROSS), bf16),
            pltpu.VMEM((32, CROSS), f32),
            pltpu.VMEM((4, 8, CROSS), f32),
            pltpu.VMEM((8, PADDED), f32),
            pltpu.VMEM((16, 8, VCOLS), f32),
            pltpu.VMEM((8, PADDED), f32),
            dma(4), dma(4), dma(4), dma(4), dma(4), dma(4),
            dma(16), dma(16), dma(16), dma(16), dma(4), dma(4),
        ],
        compiler_params=pltpu.CompilerParams(
            collective_id=2, has_side_effects=True, vmem_limit_bytes=40 << 20
        ),
    )(grad)


def body(
    bottom,
    hot_ids,
    hot_tables,
    cold_owner,
    cold_row,
    cold_rows,
    cold_acc,
    u_weight,
    v_weight,
    v_acc,
    cross_bias,
    head,
    labels,
):
    rep = lax.axis_index("replica")
    owner_t, row_t = cold_owner.T, cold_row.T
    turned = cold_rows.reshape(NCOLD, ROWS, E).transpose(0, 2, 1).reshape(8, PART, ROWS)
    part = lax.dynamic_index_in_dim(turned, rep, 0, keepdims=False).astype(bf16)
    u_full, v_half = (
        lax.all_gather(u_weight, "replica", axis=0, tiled=True),
        lax.all_gather(v_weight.astype(bf16), "replica", axis=0, tiled=True),
    )
    pooled_t, asked = forward_call(owner_t, row_t, part)
    pooled = pooled_t.T
    hot_one = (hot_ids[:, :, None] == jnp.arange(128, dtype=i32)[None, None, :]).astype(bf16)
    hot = jnp.einsum("bjv,jve->bje", hot_one, hot_tables, preferred_element_type=f32).astype(bf16)
    first = jnp.concatenate([bottom, pooled, hot.reshape(B, NHOT * E)], axis=1)
    low = jnp.dot(first, u_full, preferred_element_type=f32).astype(bf16)
    mixing = jnp.dot(low, v_half, preferred_element_type=f32) + cross_bias[None, :]
    wide = first.astype(f32)
    crossed = wide * mixing + wide
    logit = jnp.sum(crossed * head[None, :], axis=1)
    dlogit = jax.nn.sigmoid(logit) - labels.astype(f32)
    dcross = dlogit[:, None] * head[None, :]
    dmix = (dcross * wide).astype(bf16)
    grad_local = lax.dot_general(low, dmix, (((0,), (0,)), ((), ())), preferred_element_type=f32)
    dlow = lax.dot_general(dmix, v_half, NT, preferred_element_type=f32).astype(bf16)
    span_end = E + WIDE
    dpool = dcross[:, E:span_end] * (mixing[:, E:span_end] + 1.0)
    dpool = dpool + lax.dot_general(dlow, u_full[E:span_end], NT, preferred_element_type=f32)
    dpool_t = dpool.T.astype(bf16).astype(f32)
    grad_rows = backward_call(owner_t, dpool_t, asked)
    grad_rows = grad_rows.reshape(NCOLD, E, ROWS).transpose(0, 2, 1).reshape(NCOLD * ROWS, E)
    new_cold_acc = cold_acc + jnp.mean(grad_rows * grad_rows, axis=1)
    new_cold_rows = cold_rows - row_rate * grad_rows / (jnp.sqrt(new_cold_acc)[:, None] + eps_value)
    grad_mine = dense_call(grad_local.astype(bf16).reshape(8, 32, CROSS))
    acc_dense = v_acc + jnp.mean(grad_mine * grad_mine, axis=1)
    new_v = v_weight - dense_rate * grad_mine / (jnp.sqrt(acc_dense)[:, None] + eps_value)
    return (new_cold_rows, new_cold_acc, new_v)


def solution(mesh):
    return jax.shard_map(
        body,
        mesh=mesh,
        in_specs=(
            P(("table", "replica"), None),
            P(("table", "replica"), None),
            P(),
            P(("table", "replica"), None),
            P(("table", "replica"), None),
            P("table", None),
            P("table"),
            P("replica", None),
            P("replica", None),
            P("replica"),
            P(),
            P(),
            P(("table", "replica")),
        ),
        out_specs=(P("table", None), P("table"), P("replica", None)),
        check_vma=False,
    )
```

time: 914 us -> 296 us (0.32)
  the two profiles are of different devices: /device:TPU:8 before, /device:TPU:2 now
where the time goes in v1:
time: 296 us; the launch traced here: 295 us
  Pallas kernels  245 us (83%)
  matrix products  20.7 us (7%)
  between operations  14.3 us (5%)
  other arithmetic  9.15 us (3%)
  local copies, waits for them, and re-layouts  4.93 us (2%)
    pallas_call x1, Pallas kernels, backward_call(): pl.pallas_call(backward_kernel, out_shape=jax.ShapeDtypeStruct((8, PART,...  106 us
    pallas_call x1, Pallas kernels, forward_call(): pl.pallas_call(forward_kernel, out_shape=(jax.ShapeDtypeStruct((WIDE, B),...  82.1 us
    pallas_call x1, Pallas kernels, dense_call(): pl.pallas_call(dense_kernel, out_shape=jax.ShapeDtypeStruct((32, CROSS),...  57.6 us
    dot_general x1, matrix products, body(): jnp.dot(low, v_half, preferred_element_type=f32) + cross_bias[None, :]  7.4 us
  transfers between devices with their start and end apart: 2, of which 0 were waited for; matrix products, arithmetic and copies ran while one was open for 3% of the time, Pallas kernels for 28%

profile of v1, /device:TPU:2, one launch (start us, length us, event | category | flops | bytes accessed | tf_op | source)
XLA Modules:
  0.0 295.4 jit_solution(5965883286058676213)
XLA Ops:
  7.2 0.0 copy-start
  7.2 0.0 copy-start.10
  7.2 0.0 all-gather.3.cloned.1.call-start
  7.2 0.7 all-gather.3.cloned.1.call-update
  7.9 0.0 all-gather.5.cloned.1.call-start
  8.0 1.7 convert_element_type.48
  9.7 0.0 all-gather.5.cloned.1.call-update
  9.7 1.3 copy.16
  11.0 0.9 copy.18
  12.0 0.0 copy-start.1
  12.0 0.7 copy-done.1
  12.7 0.7 copy-done.3
  13.4 82.1 %shard_map.148 = (bf16[768,256]{1,0:T(8,128)(2,1)S(1)}, s32[64,8,128]{2,1,0:T(8,128)S(1)}) custom-call(s32[12,256]{1,0:T(8,128)S(1)} %bitcast.30, s32[12,256]{1,0:T(8,128)S(1)} %bitcast.32, bf16[96,256]{1,0:T(8,128)(2,1)S(1)} %fusion.15.part_ref), custom_call_target="tpu_custom_call" | custom-call | tf_op jit(solution)/shard_map/pallas_call | solution.py:745
  95.5 0.0 copy-done
  95.5 0.0 copy-done.10
  95.6 0.0 copy-start.4
  95.6 1.9 fusion.4
  97.5 0.0 copy-start.8
  97.5 0.0 all-gather.3.cloned.1.call-done
  97.5 0.0 copy-start.11
  97.5 0.0 copy-start.15
  97.5 2.6 convolution_convert_fusion.2
  100.2 0.0 copy-start.14
  100.2 0.0 all-gather.5.cloned.1.call-done
  100.2 0.0 copy-done.8
  100.2 0.0 copy-done.11
  100.2 0.0 copy-done.15
  100.2 7.4 %fusion.2 = (f32[256]{0:T(256)S(1)}, f32[256,3456]{0,1:T(8,128)}) fusion(f32[3456]{0:T(1024)S(1)} %copy-done.11, bf16[256,2560]{0,1:T(8,128)(2,1)S(1)} %bitcast.41, bf16[256,768]{0,1:T(8,128)(2,1)S(1)} %bitcast.34, bf16[256,128]{0,1:T(8,128)(2,1)S(1)} %copy.18, f32[3456]{0:T(1024)S(1)} %copy-done.15, bf16[256,256]{1,0:T(8,128)(2,1)S(1)} %convolution_convert_fusion.2, ...), kind=kOutput, calls=%fused_computation.6 | convolution fusion | flops 462716672 | bytes 7237632 | tf_op jit(solution)/shard_map/dot_general | solution.py:848
  107.6 0.0 copy-done.14
  107.7 0.0 copy-start.13
  107.7 2.3 broadcast_multiply_fusion
  110.0 0.0 copy-done.4
  110.0 0.0 copy-done.9
  110.0 4.5 %convolution_convert_fusion = bf16[256,3456]{1,0:T(8,128)(2,1)S(1)} fusion(bf16[256,256]{1,0:T(8,128)(2,1)S(1)} %convolution_convert_fusion.2, f32[3456]{0:T(1024)S(1)} %copy-done.11, f32[256]{0:T(256)S(1)} %divide_subtract_fusion.1, bf16[256,2560]{0,1:T(8,128)(2,1)S(1)} %bitcast.43, bf16[256,768]{0,1:T(8,128)(2,1)S(1)} %bitcast.35, ...), kind=kOutput, calls=%fused_computation.2 | convolution fusion | flops 461832192 | bytes 3684864 | tf_op jit(solution)/shard_map/dot_general | solution.py:855
  114.5 0.0 copy-start.2
  114.5 4.3 %fusion.8.dpool_ref = f32[768,256]{1,0:T(8,128)S(1)} fusion(bf16[256,3456]{1,0:T(8,128)(2,1)} %all-gather.5.cloned.1.call-done, f32[3456]{0:T(1024)} %param.24, f32[256]{0:T(256)} %copy-done.13, f32[256,3456]{0,1:T(8,128)} %get-tuple-element.12, f32[256,3456]{0,1:T(8,128)} %broadcast_multiply_fusion, bf16[3456,256]{1,0:T(8,128)(2,1)} %all-gather.3.cloned.1.call-done, ...), kind=kOutput, calls=%fused_computation.16 | convolution fusion | flops 562659328 | bytes 6308864 | tf_op jit(solution)/shard_map/dot_general | solution.py:859
  118.8 105.7 %shard_map.149 = f32[8,96,256]{2,1,0:T(8,128)S(1)} custom-call(s32[12,256]{1,0:T(8,128)S(1)} %bitcast.31, f32[768,256]{1,0:T(8,128)S(1)} %fusion.8.dpool_ref, s32[64,8,128]{2,1,0:T(8,128)S(1)} %get-tuple-element.6.asked_ref), custom_call_target="tpu_custom_call" | custom-call | tf_op jit(solution)/shard_map/pallas_call | solution.py:773
  224.6 1.0 broadcast_multiply_fusion.1
  225.6 1.2 copy.21
  226.8 1.3 reduce_sum.28
  228.1 0.0 copy-start.7
  228.1 0.0 copy-start.6
  228.1 57.6 %shard_map.150 = f32[32,3456]{1,0:T(8,128)S(1)} custom-call(bf16[8,32,3456]{2,1,0:T(8,128)(2,1)S(1)} %bitcast.29), custom_call_target="tpu_custom_call" | custom-call | tf_op jit(solution)/shard_map/pallas_call | solution.py:796
  285.7 0.1 multiply_reduce_fusion
  285.9 0.9 divide_subtract_fusion
  286.8 0.6 sqrt_add_fusion
  287.4 0.0 copy-done.6
  287.4 1.2 fusion.13
  (16 shorter events, 0.1 us)
Async XLA Ops:
  7.2 88.4 %copy-start = (bf16[20,128,128]{2,1,0:T(8,128)(2,1)S(1)}, bf16[20,128,128]{2,1,0:T(8,128)(2,1)}, u32[]{:S(2)}) copy-start(bf16[20,128,128]{2,1,0:T(8,128)(2,1)} %param.15) | copy-start | bytes 1966084
  7.2 88.4 %copy-start.10 = (s32[256,20]{0,1:T(8,128)S(1)}, s32[256,20]{0,1:T(8,128)}, u32[]{:S(2)}) copy-start(s32[256,20]{0,1:T(8,128)} %param.14) | copy-start | bytes 61444
  7.2 90.3 %all-gather.3.cloned.1.call-start = ((), (), s32[]{:S(2)}) async-start(), calls=%async_computation | async-start | bytes 1990656 | tf_op jit(solution)/shard_map/all_gather | solution.py:839
  7.9 92.3 %all-gather.5.cloned.1.call-start = ((), (), s32[]{:S(2)}) async-start(), calls=%async_computation.1 | async-start | bytes 1990656 | tf_op jit(solution)/shard_map/all_gather | solution.py:840
  12.0 0.7 copy-start.1
  12.7 0.7 copy-start.3
  95.6 14.4 %copy-start.4 = (bf16[768,256]{1,0:T(8,128)(2,1)}, bf16[768,256]{1,0:T(8,128)(2,1)S(1)}, u32[]{:S(2)}) copy-start(bf16[768,256]{1,0:T(8,128)(2,1)S(1)} %get-tuple-element.5) | copy-start | bytes 1179652
  97.5 2.7 copy-start.8
  97.5 2.7 copy-start.11
  97.5 2.7 copy-start.15
  100.2 7.5 %copy-start.14 = (s32[256]{0:T(256)S(1)}, s32[256]{0:T(256)}, u32[]{:S(2)}) copy-start(s32[256]{0:T(256)} %param.25) | copy-start | bytes 3076
  107.6 2.4 copy-start.9
  107.7 6.8 %copy-start.13 = (f32[256]{0:T(256)}, f32[256]{0:T(256)S(1)}, u32[]{:S(2)}) copy-start(f32[256]{0:T(256)S(1)} %divide_subtract_fusion.1) | copy-start | bytes 3076
  114.5 4.3 %copy-start.2 = (s32[256,12]{0,1:T(8,128)S(1)}, s32[256,12]{0,1:T(8,128)}, u32[]{:S(2)}) copy-start(s32[256,12]{0,1:T(8,128)} %param.16) | copy-start | bytes 36868
  225.6 60.3 %copy-start.16 = (f32[32]{0:T(128)S(1)}, f32[32]{0:T(128)}, u32[]{:S(2)}) copy-start(f32[32]{0:T(128)} %param.22) | copy-start | bytes 388
  226.8 60.0 %copy-start.12 = (f32[1536]{0:T(1024)S(1)}, f32[1536]{0:T(1024)}, u32[]{:S(2)}) copy-start(f32[1536]{0:T(1024)} %param.19) | copy-start | bytes 18436
  226.8 60.6 %copy-start.5 = (f32[1536,128]{1,0:T(8,128)S(1)}, f32[1536,128]{1,0:T(8,128)}, u32[]{:S(2)}) copy-start(f32[1536,128]{1,0:T(8,128)} %param.18) | copy-start | bytes 2359300
  228.1 57.8 %copy-start.7 = (f32[32,3456]{1,0:T(8,128)S(1)}, f32[32,3456]{1,0:T(8,128)}, u32[]{:S(2)}) copy-start(f32[32,3456]{1,0:T(8,128)} %param.21) | copy-start | bytes 1327108
  228.1 59.3 %copy-start.6 = (f32[6,256,128]{2,1,0:T(8,128)S(1)}, f32[6,256,128]{2,1,0:T(8,128)}, u32[]{:S(2)}) copy-start(f32[6,256,128]{2,1,0:T(8,128)} %copy.21) | copy-start | bytes 2359300
Sparse Core Ops, SparseCore 0:
  10.1 41.7 all-gather.2
  54.6 42.9 all-gather.4

commit v2 on v1

v2 whole, which is shorter than its diff:
```python
import functools
import jax
import jax.numpy as jnp
from jax import lax
from jax.experimental import pallas as pl
from jax.experimental.pallas import tpu as pltpu
from jax.sharding import PartitionSpec as P

NCOLD = 6
LOOK = 2
NHOT = 20
LOOKUPS = NCOLD * LOOK
E = 128
B = 256
ROWS = 256
SLOTS = 128
GROUP = 64
ITSELF = 40
PAIR_SELF = ITSELF // 2
WIDE = NCOLD * E
PART = WIDE // 8
CROSS = 3456
PADDED = 3584
COLS = 384
U_ROWS = 432
V_ROWS = 32
RANK = 256
VCHUNKS = 14
VCOLS = 256
MESH = pl.DeviceIdType.MESH

row_rate = 0.1
dense_rate = 0.05
eps_value = 1e-08

f32 = jnp.float32
bf16 = jnp.bfloat16
i32 = jnp.int32
NT = (((1,), (1,)), ((), ()))


def place_of():
    table, rep = lax.axis_index("table"), lax.axis_index("replica")
    return table // 16, table % 16, rep


def dev(y, z, rep):
    return {"table": y * 16 + z, "replica": rep}


def member_of(y, z, rep):
    return y * 16 + rep * 2 + z % 2


def member_dev(member, z):
    return dev(member // 16, z - z % 2 + member % 2, (member // 2) % 8)


def peer(i, y, z, rep):
    py = (y + 2 + i // 16) % 4
    px = (rep // 2 + 2 + (i // 4) % 4) % 4
    pc = (rep + (i // 2) % 2) % 2
    pz = (z + i) % 2
    return py * 16 + px * 4 + pc * 2 + pz


def peer_back(i, y, z, rep):
    py = (y + 6 - i // 16) % 4
    px = (rep // 2 + 6 - (i // 4) % 4) % 4
    pc = (rep + (i // 2) % 2) % 2
    pz = (z + i) % 2
    return py * 16 + px * 4 + pc * 2 + pz


def tables(owner_ref, row_ref, pos, tab, rows):
    owners = lax.broadcasted_iota(i32, (GROUP, B), 0)
    named = jnp.zeros((GROUP, B), f32)
    table = jnp.zeros((GROUP, B), f32)
    row = jnp.zeros((GROUP, B), f32)
    for k in range(LOOKUPS):
        hit = owners == owner_ref[k : k + 1, :]
        named = jnp.where(hit, 1.0, named)
        table = jnp.where(hit, float(k // LOOK), table)
        row = jnp.where(hit, row_ref[k : k + 1, :].astype(f32), row)
    before = jnp.where(
        lax.broadcasted_iota(i32, (B, B), 0) < lax.broadcasted_iota(i32, (B, B), 1), 1.0, 0.0
    ).astype(bf16)
    place = jnp.dot(named.astype(bf16), before, preferred_element_type=f32)
    pos[...] = jnp.where(named > 0.0, place, -1.0)
    tab[...] = table
    rows[...] = row


def slots_of(pos, o):
    lines = lax.broadcasted_iota(i32, (SLOTS, B), 0).astype(f32)
    return jnp.where(lines == pos[pl.ds(o, 1), :], 1.0, 0.0).astype(bf16)


def rows_of(code):
    lines = lax.broadcasted_iota(i32, (ROWS, code.shape[1]), 0)
    return jnp.where(lines == code % ROWS, 1.0, 0.0).astype(bf16)


def others(count, act):
    def step(i, carry):
        @pl.when(i != ITSELF)
        def _():
            act(i)

        return carry

    lax.fori_loop(0, count, step, 0)


def step_kernel(
    owner_ref, row_ref, part_ref, bottom_ref, ids_ref, hot_ref, u_ref, v_ref, bias_ref, head_ref, label_ref,
    grad_ref, total_ref,
    held, replies, back, ask, asked, pos, tab, rows, picks, pooled,
    u_full, v_full, first, mixed, low_t, dlow, dpool, grads,
    arrived, out, acc, part_out, part_in, whole,
    core_in, pair, x_in, mine, y_in, column, z_in, strip,
    held_send, held_recv, ask_send, ask_recv, rep_send, rep_recv, own_sem,
    w_send, w_recv, wc_send, wc_recv,
    out_send, out_recv, part_send, part_recv, all_send, all_recv,
    core_send, core_recv, x_send, x_recv, y_send, y_recv, z_send, z_recv, zb_send, zb_recv, yb_send, yb_recv,
):
    y, z, rep = place_of()
    x, c = rep // 2, rep % 2
    other_c = 1 - c
    sibling = x * 2 + other_c
    me = member_of(y, z, rep)
    home = z // 2
    owner_z = rep * 2 + z % 2
    self_holder = home == rep

    bar = pltpu.get_barrier_semaphore()

    def signal(y_, z_, rep_):
        pl.semaphore_signal(bar, inc=1, device_id=dev(y_, z_, rep_), device_id_type=MESH)

    def greet_member(i):
        pl.semaphore_signal(
            bar, inc=1, device_id=member_dev(peer(i, y, z, rep), z), device_id_type=MESH
        )

    others(GROUP, greet_member)

    def holder(j):
        return (z + 2 * j) % 16

    def source(j):
        return owner_z, (rep + j) % 8

    def greet_parts(j, carry):
        @pl.when(jnp.logical_or(holder(j) != z, home != rep))
        def _():
            signal(y, holder(j), home)

        sz, srep = source(j)

        @pl.when(jnp.logical_or(sz != z, srep != rep))
        def _():
            signal(y, sz, srep)

        return carry

    lax.fori_loop(0, 8, greet_parts, 0)

    def greet_z(k, carry):
        signal(y, (z + k) % 16, rep)
        return carry

    lax.fori_loop(1, 16, greet_z, 0)
    pl.semaphore_wait(bar, GROUP - 1 + 16 - jnp.where(self_holder, 2, 0).astype(i32) + 15)

    def part_copy(j):
        return pltpu.make_async_remote_copy(
            src_ref=part_ref,
            dst_ref=held.at[rep],
            send_sem=held_send.at[j],
            recv_sem=held_recv.at[rep],
            device_id=dev(y, holder(j), home),
            device_id_type=MESH,
        )

    def send_part(j, carry):
        @pl.when(jnp.logical_or(holder(j) != z, home != rep))
        def _():
            part_copy(j).start()

        return carry

    lax.fori_loop(0, 8, send_part, 0)
    own = pltpu.make_async_copy(part_ref, held.at[rep], own_sem.at[0])

    @pl.when(self_holder)
    def _():
        own.start()

    def u_at(r):
        return u_full.at[pl.ds(pl.multiple_of(r * U_ROWS, 16), U_ROWS), :]

    def v_at(r):
        return v_full.at[pl.ds(pl.multiple_of(r * V_ROWS, 16), V_ROWS), :]

    def weight_copies(src_u, src_v, r, sends, recvs, slot, y_, z_, rep_):
        return [
            pltpu.make_async_remote_copy(
                src_ref=src,
                dst_ref=dst,
                send_sem=sends.at[2 * slot + i],
                recv_sem=recvs.at[2 * slot + i],
                device_id=dev(y_, z_, rep_),
                device_id_type=MESH,
            )
            for i, (src, dst) in enumerate([(src_u, u_at(r)), (src_v, v_at(r))])
        ]

    w_copies = []
    for k in (2, 1, 3):
        to = ((x + k) % 4) * 2 + c
        w_copies += weight_copies(u_ref, v_ref, rep, w_send, w_recv, k, y, z, to)
    w_copies += weight_copies(u_ref, v_ref, rep, w_send, w_recv, 0, y, z, sibling)
    for copy in w_copies:
        copy.start()
    own_u = pltpu.make_async_copy(u_ref, u_at(rep), own_sem.at[1])
    own_v = pltpu.make_async_copy(v_ref, v_at(rep), own_sem.at[2])
    own_u.start()
    own_v.start()

    tables(owner_ref, row_ref, pos, tab, rows)
    lines16 = lax.broadcasted_iota(i32, (16, B), 0)

    def ask_copy(m):
        return pltpu.make_async_remote_copy(
            src_ref=ask.at[m],
            dst_ref=asked.at[me],
            send_sem=ask_send.at[m],
            recv_sem=ask_recv.at[me],
            device_id=member_dev(m, z),
            device_id_type=MESH,
        )

    def ask_pair(p, carry):
        a, b = peer(2 * p, y, z, rep), peer(2 * p + 1, y, z, rep)
        pick_a, pick_b = slots_of(pos, a), slots_of(pos, b)
        picks[a] = pick_a
        picks[b] = pick_b
        lhs = jnp.where(lines16 == 0, rows[pl.ds(a, 1), :], 0.0)
        lhs = jnp.where(lines16 == 1, tab[pl.ds(a, 1), :], lhs)
        lhs = jnp.where(lines16 == 2, rows[pl.ds(b, 1), :], lhs)
        lhs = jnp.where(lines16 == 3, tab[pl.ds(b, 1), :], lhs).astype(bf16)
        got = lax.dot_general(
            lhs, jnp.concatenate([pick_a, pick_b], axis=0), NT, preferred_element_type=f32
        )
        code_a = (got[0:1, :SLOTS] + got[1:2, :SLOTS] * float(ROWS)).astype(i32)
        code_b = (got[2:3, SLOTS:] + got[3:4, SLOTS:] * float(ROWS)).astype(i32)
        ask[a] = jnp.broadcast_to(code_a, (8, SLOTS))
        ask[b] = jnp.broadcast_to(code_b, (8, SLOTS))

        @pl.when(p != PAIR_SELF)
        def _():
            ask_copy(a).start()

        @pl.when(p == PAIR_SELF)
        def _():
            asked[me] = ask[me]

        ask_copy(b).start()
        return carry

    lax.fori_loop(0, GROUP // 2, ask_pair, 0)

    first[:, 0:E] = bottom_ref[...]
    lanes = lax.broadcasted_iota(i32, (B, E), 1)
    for j in range(NHOT):
        one = jnp.where(lanes == ids_ref[:, j : j + 1], 1.0, 0.0).astype(bf16)
        at = E + WIDE + j * E
        first[:, at : at + E] = jnp.dot(one, hot_ref[j], preferred_element_type=f32).astype(bf16)

    wc_copies = []
    for k in (1, 3, 2):
        came = ((x + 4 - k) % 4) * 2 + c
        for copy in weight_copies(u_at(came), v_at(came), came, w_send, w_recv, k, y, z, came):
            copy.wait_recv()
        forward = weight_copies(u_at(came), v_at(came), came, wc_send, wc_recv, k, y, z, sibling)
        for copy in forward:
            copy.start()
        wc_copies += forward

    def await_part(j, carry):
        sz, srep = source(j)

        @pl.when(jnp.logical_or(sz != z, srep != rep))
        def _():
            pltpu.make_async_remote_copy(
                src_ref=part_ref,
                dst_ref=held.at[srep],
                send_sem=held_send.at[0],
                recv_sem=held_recv.at[srep],
                device_id=dev(y, sz, srep),
                device_id_type=MESH,
            ).wait_recv()

        return carry

    lax.fori_loop(0, 8, await_part, 0)

    @pl.when(self_holder)
    def _():
        own.wait()

    def reply_copy(m):
        return pltpu.make_async_remote_copy(
            src_ref=back.at[m],
            dst_ref=replies.at[me],
            send_sem=rep_send.at[m],
            recv_sem=rep_recv.at[me],
            device_id=member_dev(m, z),
            device_id_type=MESH,
        )

    def await_ask(m):
        pltpu.make_async_remote_copy(
            src_ref=ask.at[m],
            dst_ref=asked.at[m],
            send_sem=ask_send.at[m],
            recv_sem=ask_recv.at[m],
            device_id=member_dev(m, z),
            device_id_type=MESH,
        ).wait_recv()

    def reply_pair(p, carry):
        a, b = peer_back(2 * p, y, z, rep), peer_back(2 * p + 1, y, z, rep)

        @pl.when(p != PAIR_SELF)
        def _():
            await_ask(a)

        await_ask(b)
        code = jnp.concatenate([asked[a][0:1, :], asked[b][0:1, :]], axis=1)
        table = code // ROWS
        found = jnp.dot(
            held[...].reshape(WIDE, ROWS), rows_of(code), preferred_element_type=f32
        )
        got = found[0:E]
        for t in range(1, NCOLD):
            got = jnp.where(table == t, found[t * E : (t + 1) * E], got)
        got = got.astype(bf16)
        back[a] = got[:, :SLOTS]
        back[b] = got[:, SLOTS:]

        @pl.when(p != PAIR_SELF)
        def _():
            reply_copy(a).start()

        @pl.when(p == PAIR_SELF)
        def _():
            replies[me] = back[me]

        reply_copy(b).start()
        return carry

    lax.fori_loop(0, GROUP // 2, reply_pair, 0)

    for k in range(4):
        came = ((x + 4 - k) % 4) * 2 + other_c
        sends, recvs = (w_send, w_recv) if k == 0 else (wc_send, wc_recv)
        for copy in weight_copies(u_at(came), v_at(came), came, sends, recvs, k, y, z, sibling):
            copy.wait_recv()
    own_u.wait()
    own_v.wait()
    hot_at = E + WIDE
    low = jnp.dot(first[:, 0:E], u_full[0:E, :], preferred_element_type=f32)
    low = low + jnp.dot(first[:, hot_at:], u_full[hot_at:, :], preferred_element_type=f32)

    pooled[...] = jnp.zeros((WIDE, B), f32)

    def await_reply(m):
        pltpu.make_async_remote_copy(
            src_ref=back.at[m],
            dst_ref=replies.at[m],
            send_sem=rep_send.at[m],
            recv_sem=rep_recv.at[m],
            device_id=member_dev(m, z),
            device_id_type=MESH,
        ).wait_recv()

    def pool_pair(p, carry):
        a, b = peer(2 * p, y, z, rep), peer(2 * p + 1, y, z, rep)

        @pl.when(p != PAIR_SELF)
        def _():
            await_reply(a)

        await_reply(b)
        got_a = jnp.dot(replies[a], picks[a], preferred_element_type=f32)
        got_b = jnp.dot(replies[b], picks[b], preferred_element_type=f32)
        tab_a, tab_b = tab[pl.ds(a, 1), :], tab[pl.ds(b, 1), :]
        for t in range(NCOLD):
            more = jnp.where(tab_a == float(t), got_a, 0.0) + jnp.where(
                tab_b == float(t), got_b, 0.0
            )
            pooled[t * E : (t + 1) * E, :] += more
        return carry

    lax.fori_loop(0, GROUP // 2, pool_pair, 0)
    for t in range(NCOLD):
        first[:, E + t * E : E + (t + 1) * E] = pooled[t * E : (t + 1) * E, :].T.astype(bf16)

    low = low + jnp.dot(first[:, E:hot_at], u_full[E:hot_at, :], preferred_element_type=f32)
    low_half = low.astype(bf16)
    low_t[...] = low.T.astype(bf16)

    def cols(i, width):
        return pl.ds(pl.multiple_of(i * width, width), width)

    def forward_cols(i, sums):
        at = cols(i, COLS)
        mixing = jnp.dot(low_half, v_full[:, at], preferred_element_type=f32) + bias_ref[:, at]
        wide = first[:, at].astype(f32)
        crossed = (wide * mixing + wide) * head_ref[:, at]
        mixed[:, at] = mixing
        for q in range(COLS // E):
            sums = sums + crossed[:, q * E : (q + 1) * E]
        return sums

    sums = lax.fori_loop(0, CROSS // COLS, forward_cols, jnp.zeros((B, E), f32))
    logit = jnp.sum(sums, axis=1, keepdims=True)
    dlogit = jax.nn.sigmoid(logit) - label_ref[...].astype(f32)

    dlow[...] = jnp.zeros((B, RANK), f32)

    def backward_cols(i, carry):
        at = cols(i, COLS)
        dmix = (dlogit * head_ref[:, at] * first[:, at].astype(f32)).astype(bf16)
        dlow[...] += lax.dot_general(dmix, v_full[:, at], NT, preferred_element_type=f32)
        grads[:, at] = jnp.dot(low_t[...], dmix, preferred_element_type=f32).astype(bf16)
        return carry

    lax.fori_loop(0, CROSS // COLS, backward_cols, 0)
    dlow_half = dlow[...].astype(bf16)
    for t in range(NCOLD):
        lo, hi = E + t * E, E + (t + 1) * E
        direct = dlogit * head_ref[:, lo:hi] * (mixed[:, lo:hi] + 1.0)
        through = lax.dot_general(u_full[lo:hi, :], dlow_half, NT, preferred_element_type=f32)
        dpool[t * E : (t + 1) * E, :] = (direct.T + through).astype(bf16).astype(f32)

    def v_rows(r):
        return pl.ds(pl.multiple_of(r * V_ROWS, V_ROWS), V_ROWS)

    core_copies = []
    for k in range(4):
        copy = pltpu.make_async_remote_copy(
            src_ref=grads.at[v_rows(2 * k + other_c), :],
            dst_ref=core_in.at[k],
            send_sem=core_send.at[k],
            recv_sem=core_recv.at[k],
            device_id=dev(y, z, sibling),
            device_id_type=MESH,
        )
        copy.start()
        core_copies.append(copy)

    def out_copy(m):
        return pltpu.make_async_remote_copy(
            src_ref=out.at[m],
            dst_ref=arrived.at[me],
            send_sem=out_send.at[m],
            recv_sem=out_recv.at[me],
            device_id=member_dev(m, z),
            device_id_type=MESH,
        )

    def pack(m):
        which = tab[pl.ds(m, 1), :]
        chosen = dpool[0:E, :]
        for t in range(1, NCOLD):
            chosen = jnp.where(which == float(t), dpool[t * E : (t + 1) * E, :], chosen)
        out[m] = lax.dot_general(
            chosen.astype(bf16), picks[m], NT, preferred_element_type=f32
        ).astype(bf16)

    def pack_pair(p, carry):
        a, b = peer(2 * p, y, z, rep), peer(2 * p + 1, y, z, rep)
        pack(a)
        pack(b)

        @pl.when(p != PAIR_SELF)
        def _():
            out_copy(a).start()

        @pl.when(p == PAIR_SELF)
        def _():
            arrived[me] = out[me]

        out_copy(b).start()
        return carry

    lax.fori_loop(0, GROUP // 2, pack_pair, 0)

    for k in range(4):
        core_copies[k].wait_recv()
        pair[k] = (
            grads[v_rows(2 * k + c), :].astype(f32) + core_in[k].astype(f32)
        ).astype(bf16)
    x_copies = []
    for k in (2, 1, 3):
        to = (x + k) % 4
        copy = pltpu.make_async_remote_copy(
            src_ref=pair.at[to],
            dst_ref=x_in.at[k],
            send_sem=x_send.at[k],
            recv_sem=x_recv.at[k],
            device_id=dev(y, z, to * 2 + c),
            device_id_type=MESH,
        )
        copy.start()
        x_copies.append(copy)

    acc[...] = jnp.zeros((WIDE, ROWS), f32)

    def await_out(m):
        pltpu.make_async_remote_copy(
            src_ref=out.at[m],
            dst_ref=arrived.at[m],
            send_sem=out_send.at[m],
            recv_sem=out_recv.at[m],
            device_id=member_dev(m, z),
            device_id_type=MESH,
        ).wait_recv()

    def add_pair(p, carry):
        a, b = peer_back(2 * p, y, z, rep), peer_back(2 * p + 1, y, z, rep)

        @pl.when(p != PAIR_SELF)
        def _():
            await_out(a)

        await_out(b)
        code = jnp.concatenate([asked[a][0:1, :], asked[b][0:1, :]], axis=1)
        table = code // ROWS
        came = jnp.concatenate([arrived[a], arrived[b]], axis=1).astype(f32)
        lhs = jnp.concatenate(
            [jnp.where(table == t, came, 0.0).astype(bf16) for t in range(NCOLD)], axis=0
        )
        acc[...] += lax.dot_general(lhs, rows_of(code), NT, preferred_element_type=f32)
        return carry

    lax.fori_loop(0, GROUP // 2, add_pair, 0)

    def sum_copy(j):
        return pltpu.make_async_remote_copy(
            src_ref=part_out.at[j],
            dst_ref=part_in.at[home],
            send_sem=part_send.at[j],
            recv_sem=part_recv.at[home],
            device_id=dev(y, owner_z, j),
            device_id_type=MESH,
        )

    def send_sum(j, carry):
        part_out[j] = acc[pl.ds(pl.multiple_of(j * PART, PART), PART), :].astype(bf16)
        other = jnp.logical_or(owner_z != z, j != rep)

        @pl.when(other)
        def _():
            sum_copy(j).start()

        @pl.when(jnp.logical_not(other))
        def _():
            part_in[home] = part_out[j]

        return carry

    lax.fori_loop(0, 8, send_sum, 0)

    for copy in x_copies:
        copy.wait_recv()
    mine[...] = (
        pair[x].astype(f32) + x_in[1].astype(f32) + x_in[2].astype(f32) + x_in[3].astype(f32)
    )

    def band(j):
        return pl.ds(pl.multiple_of(j * 8, 8), 8)

    y_copies = []
    for k in (2, 1, 3):
        to = (y + k) % 4
        copy = pltpu.make_async_remote_copy(
            src_ref=mine.at[band(to), :],
            dst_ref=y_in.at[k],
            send_sem=y_send.at[k],
            recv_sem=y_recv.at[k],
            device_id=dev(to, z, rep),
            device_id_type=MESH,
        )
        copy.start()
        y_copies.append(copy)
    for copy in y_copies:
        copy.wait_recv()
    column[:, CROSS:] = jnp.zeros((8, PADDED - CROSS), f32)
    column[:, :CROSS] = mine[band(y), :] + y_in[1] + y_in[2] + y_in[3]

    def z_copy(k):
        to = (z + k) % 16
        return pltpu.make_async_remote_copy(
            src_ref=column.at[:, cols(to, VCOLS)],
            dst_ref=z_in.at[k],
            send_sem=z_send.at[k],
            recv_sem=z_recv.at[k],
            device_id=dev(y, to, rep),
            device_id_type=MESH,
        )

    def z_start(k, carry):
        @pl.when((z + k) % 16 < VCHUNKS)
        def _():
            z_copy(k).start()

        return carry

    lax.fori_loop(1, 16, z_start, 0)

    def await_sum(j, carry):
        sz = holder(j)

        @pl.when(jnp.logical_or(sz != z, home != rep))
        def _():
            pltpu.make_async_remote_copy(
                src_ref=part_out.at[0],
                dst_ref=part_in.at[sz // 2],
                send_sem=part_send.at[0],
                recv_sem=part_recv.at[sz // 2],
                device_id=dev(y, sz, home),
                device_id_type=MESH,
            ).wait_recv()

        return carry

    lax.fori_loop(0, 8, await_sum, 0)
    total = part_in[0].astype(f32)
    for g in range(1, 8):
        total = total + part_in[g].astype(f32)
    whole[rep] = total.astype(bf16)

    def all_copy(j):
        return pltpu.make_async_remote_copy(
            src_ref=whole.at[rep],
            dst_ref=whole.at[rep],
            send_sem=all_send.at[j],
            recv_sem=all_recv.at[rep],
            device_id=dev(y, z, (rep + j) % 8),
            device_id_type=MESH,
        )

    def send_all(j, carry):
        all_copy(j).start()
        return carry

    lax.fori_loop(1, 8, send_all, 0)

    def zb_copy(k):
        return pltpu.make_async_remote_copy(
            src_ref=strip.at[:, cols(z, VCOLS)],
            dst_ref=strip.at[:, cols(z, VCOLS)],
            send_sem=zb_send.at[k],
            recv_sem=zb_recv.at[z],
            device_id=dev(y, (z + k) % 16, rep),
            device_id_type=MESH,
        )

    @pl.when(z < VCHUNKS)
    def _():
        def z_wait(k, carry):
            pltpu.make_async_remote_copy(
                src_ref=z_in.at[k],
                dst_ref=z_in.at[k],
                send_sem=z_send.at[k],
                recv_sem=z_recv.at[k],
                device_id=dev(y, (z + 16 - k) % 16, rep),
                device_id_type=MESH,
            ).wait_recv()
            return carry

        lax.fori_loop(1, 16, z_wait, 0)
        summed = column[:, cols(z, VCOLS)]
        for k in range(1, 16):
            summed = summed + z_in[k]
        strip[:, cols(z, VCOLS)] = summed

        def zb_start(k, carry):
            zb_copy(k).start()
            return carry

        lax.fori_loop(1, 16, zb_start, 0)

    def zb_wait(k, carry):
        other = (z + 16 - k) % 16

        @pl.when(other < VCHUNKS)
        def _():
            pltpu.make_async_remote_copy(
                src_ref=strip.at[:, cols(other, VCOLS)],
                dst_ref=strip.at[:, cols(other, VCOLS)],
                send_sem=zb_send.at[k],
                recv_sem=zb_recv.at[other],
                device_id=dev(y, other, rep),
                device_id_type=MESH,
            ).wait_recv()

        return carry

    lax.fori_loop(1, 16, zb_wait, 0)

    total_ref[band(y), :] = strip[:, :CROSS]
    yb_copies = []
    for k in (2, 1, 3):
        copy = pltpu.make_async_remote_copy(
            src_ref=total_ref.at[band(y), :],
            dst_ref=total_ref.at[band(y), :],
            send_sem=yb_send.at[k],
            recv_sem=yb_recv.at[k],
            device_id=dev((y + k) % 4, z, rep),
            device_id_type=MESH,
        )
        copy.start()
        yb_copies.append(copy)

    def await_all(j, carry):
        other = (rep + 8 - j) % 8
        pltpu.make_async_remote_copy(
            src_ref=whole.at[other],
            dst_ref=whole.at[other],
            send_sem=all_send.at[j],
            recv_sem=all_recv.at[other],
            device_id=dev(y, z, other),
            device_id_type=MESH,
        ).wait_recv()
        return carry

    lax.fori_loop(1, 8, await_all, 0)
    grad_ref[...] = whole[...].astype(f32)
    for k in (2, 1, 3):
        came = band((y + 4 - k) % 4)
        pltpu.make_async_remote_copy(
            src_ref=total_ref.at[came, :],
            dst_ref=total_ref.at[came, :],
            send_sem=yb_send.at[k],
            recv_sem=yb_recv.at[k],
            device_id=dev((y + 4 - k) % 4, z, rep),
            device_id_type=MESH,
        ).wait_recv()

    for copy in w_copies + wc_copies + core_copies + x_copies + y_copies + yb_copies:
        copy.wait_send()

    def drain(i):
        m = peer(i, y, z, rep)
        ask_copy(m).wait_send()
        reply_copy(m).wait_send()
        out_copy(m).wait_send()

    others(GROUP, drain)

    def drain_parts(j, carry):
        @pl.when(jnp.logical_or(holder(j) != z, home != rep))
        def _():
            part_copy(j).wait_send()

        @pl.when(jnp.logical_or(owner_z != z, j != rep))
        def _():
            sum_copy(j).wait_send()

        return carry

    lax.fori_loop(0, 8, drain_parts, 0)

    def drain_all(j, carry):
        all_copy(j).wait_send()
        return carry

    lax.fori_loop(1, 8, drain_all, 0)

    def drain_z(k, carry):
        @pl.when((z + k) % 16 < VCHUNKS)
        def _():
            z_copy(k).wait_send()

        @pl.when(z < VCHUNKS)
        def _():
            zb_copy(k).wait_send()

        return carry

    lax.fori_loop(1, 16, drain_z, 0)


def vmem():
    return pl.BlockSpec(memory_space=pltpu.VMEM)


def dma(n):
    return pltpu.SemaphoreType.DMA((n,))


def step_call(*args):
    return pl.pallas_call(
        step_kernel,
        out_shape=(
            jax.ShapeDtypeStruct((8, PART, ROWS), f32),
            jax.ShapeDtypeStruct((V_ROWS, CROSS), f32),
        ),
        in_specs=[vmem()] * 11,
        out_specs=(vmem(), vmem()),
        scratch_shapes=[
            pltpu.VMEM((8, PART, ROWS), bf16),
            pltpu.VMEM((GROUP, E, SLOTS), bf16),
            pltpu.VMEM((GROUP, E, SLOTS), bf16),
            pltpu.VMEM((GROUP, 8, SLOTS), i32),
            pltpu.VMEM((GROUP, 8, SLOTS), i32),
            pltpu.VMEM((GROUP, B), f32),
            pltpu.VMEM((GROUP, B), f32),
            pltpu.VMEM((GROUP, B), f32),
            pltpu.VMEM((GROUP, SLOTS, B), bf16),
            pltpu.VMEM((WIDE, B), f32),
            pltpu.VMEM((CROSS, RANK), bf16),
            pltpu.VMEM((RANK, CROSS), bf16),
            pltpu.VMEM((B, CROSS), bf16),
            pltpu.VMEM((B, CROSS), f32),
            pltpu.VMEM((RANK, B), bf16),
            pltpu.VMEM((B, RANK), f32),
            pltpu.VMEM((WIDE, B), f32),
            pltpu.VMEM((RANK, CROSS), bf16),
            pltpu.VMEM((GROUP, E, SLOTS), bf16),
            pltpu.VMEM((GROUP, E, SLOTS), bf16),
            pltpu.VMEM((WIDE, ROWS), f32),
            pltpu.VMEM((8, PART, ROWS), bf16),
            pltpu.VMEM((8, PART, ROWS), bf16),
            pltpu.VMEM((8, PART, ROWS), bf16),
            pltpu.VMEM((4, V_ROWS, CROSS), bf16),
            pltpu.VMEM((4, V_ROWS, CROSS), bf16),
            pltpu.VMEM((4, V_ROWS, CROSS), bf16),
            pltpu.VMEM((V_ROWS, CROSS), f32),
            pltpu.VMEM((4, 8, CROSS), f32),
            pltpu.VMEM((8, PADDED), f32),
            pltpu.VMEM((16, 8, VCOLS), f32),
            pltpu.VMEM((8, PADDED), f32),
            dma(8), dma(8), dma(GROUP), dma(GROUP), dma(GROUP), dma(GROUP), dma(3),
            dma(8), dma(8), dma(8), dma(8),
            dma(GROUP), dma(GROUP), dma(8), dma(8), dma(8), dma(8),
            dma(4), dma(4), dma(4), dma(4), dma(4), dma(4),
            dma(16), dma(16), dma(16), dma(16), dma(4), dma(4),
        ],
        compiler_params=pltpu.CompilerParams(
            collective_id=0, has_side_effects=True, vmem_limit_bytes=56 << 20
        ),
    )(*args)


def body(
    bottom,
    hot_ids,
    hot_tables,
    cold_owner,
    cold_row,
    cold_rows,
    cold_acc,
    u_weight,
    v_weight,
    v_acc,
    cross_bias,
    head,
    labels,
):
    rep = lax.axis_index("replica")
    turned = cold_rows.reshape(NCOLD, ROWS, E).transpose(0, 2, 1).reshape(8, PART, ROWS)
    part = lax.dynamic_index_in_dim(turned, rep, 0, keepdims=False).astype(bf16)
    grad_rows, grad_mine = step_call(
        cold_owner.T, cold_row.T, part, bottom, hot_ids, hot_tables, u_weight,
        v_weight.astype(bf16), cross_bias[None, :], head[None, :], labels[:, None],
    )
    grad_rows = grad_rows.reshape(NCOLD, E, ROWS).transpose(0, 2, 1).reshape(NCOLD * ROWS, E)
    new_cold_acc = cold_acc + jnp.mean(grad_rows * grad_rows, axis=1)
    new_cold_rows = cold_rows - row_rate * grad_rows / (jnp.sqrt(new_cold_acc)[:, None] + eps_value)
    acc_dense = v_acc + jnp.mean(grad_mine * grad_mine, axis=1)
    new_v = v_weight - dense_rate * grad_mine / (jnp.sqrt(acc_dense)[:, None] + eps_value)
    return (new_cold_rows, new_cold_acc, new_v)


def solution(mesh):
    return jax.shard_map(
        body,
        mesh=mesh,
        in_specs=(
            P(("table", "replica"), None),
            P(("table", "replica"), None),
            P(),
            P(("table", "replica"), None),
            P(("table", "replica"), None),
            P("table", None),
            P("table"),
            P("replica", None),
            P("replica", None),
            P("replica"),
            P(),
            P(),
            P(("table", "replica")),
        ),
        out_specs=(P("table", None), P("table"), P("replica", None)),
        check_vma=False,
    )
```

time: 296 us -> 228 us (0.77)
  Pallas kernels: 245 us -> 213 us
  matrix products: 20.7 us -> 0 us
  between operations: 14.3 us -> 0.75 us
    pallas_call x3 -> x1, Pallas kernels: 245 us -> 213 us  [step_call(): pl.pallas_call(step_kernel, out_shape=(jax.ShapeDtypeStruct((8, PART, ROW...]
    dot_general x5 -> x0, matrix products: 20.7 us -> none  [the longest x1 7.4 us: body(): jnp.dot(low, v_half, preferred_element_type=f32) + cross_bias[None, :]]
    broadcast_in_dim x0 -> x3, local copies, waits for them, and re-layouts: none -> 4.18 us  [the longest x1 1.46 us: body(): labels[:, None]]
  transfers between devices with their start and end apart: 2 -> 0, of which waited for: 0 -> 0; matrix products, arithmetic and copies ran while one was open for 3% -> 0% of each run, Pallas kernels for 28% -> 0%
where the time goes in v2:
time: 228 us
  Pallas kernels  213 us (93%)
  local copies, waits for them, and re-layouts  7.43 us (3%)
  other arithmetic  6.85 us (3%)
    pallas_call x1, Pallas kernels, step_call(): pl.pallas_call(step_kernel, out_shape=(jax.ShapeDtypeStruct((8, PART, ROW...  213 us

profile of v2, /device:TPU:2, one launch (start us, length us, event | category | flops | bytes accessed | tf_op | source)
XLA Modules:
  0.0 227.8 jit_solution(9771634646533033013)
XLA Ops:
  0.6 0.0 copy-start
  0.6 1.4 broadcast_in_dim.11.bias_ref
  2.0 1.3 broadcast_in_dim.12.head_ref
  3.4 1.5 copy.20.ids_ref
  4.9 1.5 copy.21.label_ref
  6.3 1.7 convert_element_type.10.v_ref
  8.0 0.0 copy-done
  8.0 0.2 copy.19
  8.2 0.6 fusion.1.part_ref
  8.8 0.0 copy-start.4
  8.9 212.8 %shard_map.148 = (f32[8,96,256]{2,1,0:T(8,128)}, f32[32,3456]{1,0:T(8,128)}) custom-call(s32[12,256]{1,0:T(8,128)} %bitcast.21, s32[12,256]{1,0:T(8,128)} %bitcast.22, bf16[96,256]{1,0:T(8,128)(2,1)} %fusion.1.part_ref, bf16[256,128]{1,0:T(8,128)(2,1)} %bottom_ref.1, s32[256,20]{1,0:T(8,128)} %copy.20.ids_ref, bf16[20,128,128]{2,1,0:T(8,128)(2,1)} %hot_ref.1, ...), custom_call_target="tpu_custom_call" | custom-call | tf_op jit(solution)/shard_map/pallas_call | solution.py:808
  221.6 0.0 copy-start.1
  221.6 0.0 copy-start.2
  221.7 1.2 multiply_reduce_fusion
  222.9 0.0 copy-done.4
  222.9 0.0 copy-done.1
  222.9 1.9 divide_subtract_fusion
  224.8 0.0 copy-done.2
  224.8 0.2 broadcast_multiply_fusion
  225.0 0.3 copy.22
  225.3 0.1 reduce_sum.18
  225.3 0.0 copy-start.3
  225.4 0.7 copy-done.3
  226.0 0.6 sqrt_add_fusion
  226.6 1.2 fusion
  (3 shorter events, 0.0 us)
Async XLA Ops:
  0.6 7.4 %copy-start = (f32[1536,128]{1,0:T(8,128)S(1)}, f32[1536,128]{1,0:T(8,128)}, u32[]{:S(2)}) copy-start(f32[1536,128]{1,0:T(8,128)} %param.18) | copy-start | bytes 2359300
  8.8 214.1 %copy-start.4 = (f32[32]{0:T(128)S(1)}, f32[32]{0:T(128)}, u32[]{:S(2)}) copy-start(f32[32]{0:T(128)} %param.22) | copy-start | bytes 388
  221.6 1.3 copy-start.1
  221.6 3.2 %copy-start.2 = (f32[8,96,256]{2,1,0:T(8,128)S(1)}, f32[8,96,256]{2,1,0:T(8,128)}, u32[]{:S(2)}) copy-start(f32[8,96,256]{2,1,0:T(8,128)} %get-tuple-element.5) | copy-start | bytes 2359300
  225.3 0.7 copy-start.3

commit v3 on v2

--- a/solution.py
+++ b/solution.py
@@ -41,35 +41,43 @@
 
 def place_of():
     table, rep = lax.axis_index("table"), lax.axis_index("replica")
-    return table // 16, table % 16, rep
+    return table >> 4, table & 15, rep
 
 
 def dev(y, z, rep):
     return {"table": y * 16 + z, "replica": rep}
 
 
+def held_z(z, rep):
+    return 2 * ((((rep & 1) << 2) + (rep >> 1) - (z >> 1)) & 7) + (z & 1)
+
+
+def holding_rep(z, owner_z):
+    at = ((owner_z >> 1) + (z >> 1)) & 7
+    return ((at & 3) << 1) + (at >> 2)
+
+
 def member_of(y, z, rep):
-    return y * 16 + rep * 2 + z % 2
+    return y * 16 + held_z(z, rep)
 
 
 def member_dev(member, z):
-    return dev(member // 16, z - z % 2 + member % 2, (member // 2) % 8)
+    mz = (z - (z & 1)) + (member & 1)
+    return dev(member >> 4, mz, holding_rep(mz, member & 15))
 
 
 def peer(i, y, z, rep):
-    py = (y + 2 + i // 16) % 4
-    px = (rep // 2 + 2 + (i // 4) % 4) % 4
-    pc = (rep + (i // 2) % 2) % 2
-    pz = (z + i) % 2
-    return py * 16 + px * 4 + pc * 2 + pz
+    px = ((rep >> 1) + 2 + (i >> 2)) & 3
+    pc = (rep + (i >> 1)) & 1
+    pz = (z - (z & 1)) + ((z + i) & 1)
+    return member_of((y + 2 + (i >> 4)) & 3, pz, px * 2 + pc)
 
 
 def peer_back(i, y, z, rep):
-    py = (y + 6 - i // 16) % 4
-    px = (rep // 2 + 6 - (i // 4) % 4) % 4
-    pc = (rep + (i // 2) % 2) % 2
-    pz = (z + i) % 2
-    return py * 16 + px * 4 + pc * 2 + pz
+    px = ((rep >> 1) + 6 - ((i >> 2) & 3)) & 3
+    pc = (rep + (i >> 1)) & 1
+    pz = (z - (z & 1)) + ((z + i) & 1)
+    return member_of((y + 6 - (i >> 4)) & 3, pz, px * 2 + pc)
 
 
 def tables(owner_ref, row_ref, pos, tab, rows):
@@ -98,7 +106,7 @@
 
 def rows_of(code):
     lines = lax.broadcasted_iota(i32, (ROWS, code.shape[1]), 0)
-    return jnp.where(lines == code % ROWS, 1.0, 0.0).astype(bf16)
+    return jnp.where(lines == code & (ROWS - 1), 1.0, 0.0).astype(bf16)
 
 
 def others(count, act):
@@ -113,9 +121,9 @@
 
 
 def step_kernel(
-    owner_ref, row_ref, part_ref, bottom_ref, ids_ref, hot_ref, u_ref, v_ref, bias_ref, head_ref, label_ref,
+    owner_ref, row_ref, part_ref, bottom_ref, ids_ref, hot_hbm, u_ref, v_wide, bias_ref, head_ref, label_ref,
     grad_ref, total_ref,
-    held, replies, back, ask, asked, pos, tab, rows, picks, pooled,
+    hot_ref, v_ref, held, replies, back, ask, asked, pos, tab, rows, picks, pooled,
     u_full, v_full, first, mixed, low_t, dlow, dpool, grads,
     arrived, out, acc, part_out, part_in, whole,
     core_in, pair, x_in, mine, y_in, column, z_in, strip,
@@ -125,13 +133,16 @@
     core_send, core_recv, x_send, x_recv, y_send, y_recv, z_send, z_recv, zb_send, zb_recv, yb_send, yb_recv,
 ):
     y, z, rep = place_of()
-    x, c = rep // 2, rep % 2
+    x, c = rep >> 1, rep & 1
     other_c = 1 - c
     sibling = x * 2 + other_c
     me = member_of(y, z, rep)
-    home = z // 2
-    owner_z = rep * 2 + z % 2
-    self_holder = home == rep
+    group = z >> 1
+    owner_z = held_z(z, rep)
+    self_holder = owner_z == z
+
+    hot_copy = pltpu.make_async_copy(hot_hbm, hot_ref, own_sem.at[3])
+    hot_copy.start()
 
     bar = pltpu.get_barrier_semaphore()
 
@@ -146,31 +157,35 @@
     others(GROUP, greet_member)
 
     def holder(j):
-        return (z + 2 * j) % 16
+        hz = (z + 2 * j) & 15
+        return hz, holding_rep(hz, z)
+
+    def is_other(at):
+        return jnp.logical_or(at[0] != z, at[1] != rep)
 
     def source(j):
-        return owner_z, (rep + j) % 8
+        return owner_z, (rep + j) & 7
 
     def greet_parts(j, carry):
-        @pl.when(jnp.logical_or(holder(j) != z, home != rep))
-        def _():
-            signal(y, holder(j), home)
-
-        sz, srep = source(j)
-
-        @pl.when(jnp.logical_or(sz != z, srep != rep))
-        def _():
-            signal(y, sz, srep)
+        @pl.when(is_other(holder(j)))
+        def _():
+            signal(y, *holder(j))
+
+        @pl.when(is_other(source(j)))
+        def _():
+            signal(y, *source(j))
 
         return carry
 
     lax.fori_loop(0, 8, greet_parts, 0)
 
     def greet_z(k, carry):
-        signal(y, (z + k) % 16, rep)
+        signal(y, (z + k) & 15, rep)
         return carry
 
     lax.fori_loop(1, 16, greet_z, 0)
+    v_ref[...] = v_wide[...].astype(bf16)
+    tables(owner_ref, row_ref, pos, tab, rows)
     pl.semaphore_wait(bar, GROUP - 1 + 16 - jnp.where(self_holder, 2, 0).astype(i32) + 15)
 
     def part_copy(j):
@@ -179,12 +194,12 @@
             dst_ref=held.at[rep],
             send_sem=held_send.at[j],
             recv_sem=held_recv.at[rep],
-            device_id=dev(y, holder(j), home),
+            device_id=dev(y, *holder(j)),
             device_id_type=MESH,
         )
 
     def send_part(j, carry):
-        @pl.when(jnp.logical_or(holder(j) != z, home != rep))
+        @pl.when(is_other(holder(j)))
         def _():
             part_copy(j).start()
 
@@ -218,7 +233,7 @@
 
     w_copies = []
     for k in (2, 1, 3):
-        to = ((x + k) % 4) * 2 + c
+        to = ((x + k) & 3) * 2 + c
         w_copies += weight_copies(u_ref, v_ref, rep, w_send, w_recv, k, y, z, to)
     w_copies += weight_copies(u_ref, v_ref, rep, w_send, w_recv, 0, y, z, sibling)
     for copy in w_copies:
@@ -228,7 +243,6 @@
     own_u.start()
     own_v.start()
 
-    tables(owner_ref, row_ref, pos, tab, rows)
     lines16 = lax.broadcasted_iota(i32, (16, B), 0)
 
     def ask_copy(m):
@@ -272,15 +286,17 @@
     lax.fori_loop(0, GROUP // 2, ask_pair, 0)
 
     first[:, 0:E] = bottom_ref[...]
-    lanes = lax.broadcasted_iota(i32, (B, E), 1)
+    hot_copy.wait()
+    ids = ids_ref[...].astype(f32).T
+    lanes = lax.broadcasted_iota(i32, (B, E), 1).astype(f32)
     for j in range(NHOT):
-        one = jnp.where(lanes == ids_ref[:, j : j + 1], 1.0, 0.0).astype(bf16)
+        one = jnp.where(lanes == ids[:, j : j + 1], 1.0, 0.0).astype(bf16)
         at = E + WIDE + j * E
         first[:, at : at + E] = jnp.dot(one, hot_ref[j], preferred_element_type=f32).astype(bf16)
 
     wc_copies = []
     for k in (1, 3, 2):
-        came = ((x + 4 - k) % 4) * 2 + c
+        came = ((x + 4 - k) & 3) * 2 + c
         for copy in weight_copies(u_at(came), v_at(came), came, w_send, w_recv, k, y, z, came):
             copy.wait_recv()
         forward = weight_copies(u_at(came), v_at(came), came, wc_send, wc_recv, k, y, z, sibling)
@@ -291,7 +307,7 @@
     def await_part(j, carry):
         sz, srep = source(j)
 
-        @pl.when(jnp.logical_or(sz != z, srep != rep))
+        @pl.when(is_other((sz, srep)))
         def _():
             pltpu.make_async_remote_copy(
                 src_ref=part_ref,
@@ -339,7 +355,7 @@
 
         await_ask(b)
         code = jnp.concatenate([asked[a][0:1, :], asked[b][0:1, :]], axis=1)
-        table = code // ROWS
+        table = code >> 8
         found = jnp.dot(
             held[...].reshape(WIDE, ROWS), rows_of(code), preferred_element_type=f32
         )
@@ -364,7 +380,7 @@
     lax.fori_loop(0, GROUP // 2, reply_pair, 0)
 
     for k in range(4):
-        came = ((x + 4 - k) % 4) * 2 + other_c
+        came = ((x + 4 - k) & 3) * 2 + other_c
         sends, recvs = (w_send, w_recv) if k == 0 else (wc_send, wc_recv)
         for copy in weight_copies(u_at(came), v_at(came), came, sends, recvs, k, y, z, sibling):
             copy.wait_recv()
@@ -415,11 +431,15 @@
     def cols(i, width):
         return pl.ds(pl.multiple_of(i * width, width), width)
 
+    def line(ref, i):
+        n = COLS // E
+        return jnp.concatenate([ref[pl.ds(i * n + q, 1), :] for q in range(n)], axis=1)
+
     def forward_cols(i, sums):
         at = cols(i, COLS)
-        mixing = jnp.dot(low_half, v_full[:, at], preferred_element_type=f32) + bias_ref[:, at]
+        mixing = jnp.dot(low_half, v_full[:, at], preferred_element_type=f32) + line(bias_ref, i)
         wide = first[:, at].astype(f32)
-        crossed = (wide * mixing + wide) * head_ref[:, at]
+        crossed = (wide * mixing + wide) * line(head_ref, i)
         mixed[:, at] = mixing
         for q in range(COLS // E):
             sums = sums + crossed[:, q * E : (q + 1) * E]
@@ -427,13 +447,15 @@
 
     sums = lax.fori_loop(0, CROSS // COLS, forward_cols, jnp.zeros((B, E), f32))
     logit = jnp.sum(sums, axis=1, keepdims=True)
-    dlogit = jax.nn.sigmoid(logit) - label_ref[...].astype(f32)
+    label = jnp.concatenate([label_ref[0:1, :], label_ref[1:2, :]], axis=1).astype(f32)
+    label = jnp.broadcast_to(label, (8, B)).T
+    dlogit = jax.nn.sigmoid(logit) - label[:, 0:1]
 
     dlow[...] = jnp.zeros((B, RANK), f32)
 
     def backward_cols(i, carry):
         at = cols(i, COLS)
-        dmix = (dlogit * head_ref[:, at] * first[:, at].astype(f32)).astype(bf16)
+        dmix = (dlogit * line(head_ref, i) * first[:, at].astype(f32)).astype(bf16)
         dlow[...] += lax.dot_general(dmix, v_full[:, at], NT, preferred_element_type=f32)
         grads[:, at] = jnp.dot(low_t[...], dmix, preferred_element_type=f32).astype(bf16)
         return carry
@@ -442,7 +464,7 @@
     dlow_half = dlow[...].astype(bf16)
     for t in range(NCOLD):
         lo, hi = E + t * E, E + (t + 1) * E
-        direct = dlogit * head_ref[:, lo:hi] * (mixed[:, lo:hi] + 1.0)
+        direct = dlogit * head_ref[t + 1 : t + 2, :] * (mixed[:, lo:hi] + 1.0)
         through = lax.dot_general(u_full[lo:hi, :], dlow_half, NT, preferred_element_type=f32)
         dpool[t * E : (t + 1) * E, :] = (direct.T + through).astype(bf16).astype(f32)
 
@@ -497,7 +519,7 @@
         out_copy(b).start()
         return carry
 
-    lax.fori_loop(0, GROUP // 2, pack_pair, 0)
+    lax.fori_loop(0, 16, pack_pair, 0)
 
     for k in range(4):
         core_copies[k].wait_recv()
@@ -506,7 +528,7 @@
         ).astype(bf16)
     x_copies = []
     for k in (2, 1, 3):
-        to = (x + k) % 4
+        to = (x + k) & 3
         copy = pltpu.make_async_remote_copy(
             src_ref=pair.at[to],
             dst_ref=x_in.at[k],
@@ -517,6 +539,9 @@
         )
         copy.start()
         x_copies.append(copy)
+
+    lax.fori_loop(16, 32, pack_pair, 0)
+
 
     acc[...] = jnp.zeros((WIDE, ROWS), f32)
 
@@ -539,7 +564,7 @@
 
         await_out(b)
         code = jnp.concatenate([asked[a][0:1, :], asked[b][0:1, :]], axis=1)
-        table = code // ROWS
+        table = code >> 8
         came = jnp.concatenate([arrived[a], arrived[b]], axis=1).astype(f32)
         lhs = jnp.concatenate(
             [jnp.where(table == t, came, 0.0).astype(bf16) for t in range(NCOLD)], axis=0
@@ -547,33 +572,7 @@
         acc[...] += lax.dot_general(lhs, rows_of(code), NT, preferred_element_type=f32)
         return carry
 
-    lax.fori_loop(0, GROUP // 2, add_pair, 0)
-
-    def sum_copy(j):
-        return pltpu.make_async_remote_copy(
-            src_ref=part_out.at[j],
-            dst_ref=part_in.at[home],
-            send_sem=part_send.at[j],
-            recv_sem=part_recv.at[home],
-            device_id=dev(y, owner_z, j),
-            device_id_type=MESH,
-        )
-
-    def send_sum(j, carry):
-        part_out[j] = acc[pl.ds(pl.multiple_of(j * PART, PART), PART), :].astype(bf16)
-        other = jnp.logical_or(owner_z != z, j != rep)
-
-        @pl.when(other)
-        def _():
-            sum_copy(j).start()
-
-        @pl.when(jnp.logical_not(other))
-        def _():
-            part_in[home] = part_out[j]
-
-        return carry
-
-    lax.fori_loop(0, 8, send_sum, 0)
+    lax.fori_loop(0, 12, add_pair, 0)
 
     for copy in x_copies:
         copy.wait_recv()
@@ -586,7 +585,7 @@
 
     y_copies = []
     for k in (2, 1, 3):
-        to = (y + k) % 4
+        to = (y + k) & 3
         copy = pltpu.make_async_remote_copy(
             src_ref=mine.at[band(to), :],
             dst_ref=y_in.at[k],
@@ -597,13 +596,14 @@
         )
         copy.start()
         y_copies.append(copy)
+    lax.fori_loop(12, 20, add_pair, 0)
     for copy in y_copies:
         copy.wait_recv()
     column[:, CROSS:] = jnp.zeros((8, PADDED - CROSS), f32)
     column[:, :CROSS] = mine[band(y), :] + y_in[1] + y_in[2] + y_in[3]
 
     def z_copy(k):
-        to = (z + k) % 16
+        to = (z + k) & 15
         return pltpu.make_async_remote_copy(
             src_ref=column.at[:, cols(to, VCOLS)],
             dst_ref=z_in.at[k],
@@ -614,7 +614,7 @@
         )
 
     def z_start(k, carry):
-        @pl.when((z + k) % 16 < VCHUNKS)
+        @pl.when((z + k) & 15 < VCHUNKS)
         def _():
             z_copy(k).start()
 
@@ -622,43 +622,7 @@
 
     lax.fori_loop(1, 16, z_start, 0)
 
-    def await_sum(j, carry):
-        sz = holder(j)
-
-        @pl.when(jnp.logical_or(sz != z, home != rep))
-        def _():
-            pltpu.make_async_remote_copy(
-                src_ref=part_out.at[0],
-                dst_ref=part_in.at[sz // 2],
-                send_sem=part_send.at[0],
-                recv_sem=part_recv.at[sz // 2],
-                device_id=dev(y, sz, home),
-                device_id_type=MESH,
-            ).wait_recv()
-
-        return carry
-
-    lax.fori_loop(0, 8, await_sum, 0)
-    total = part_in[0].astype(f32)
-    for g in range(1, 8):
-        total = total + part_in[g].astype(f32)
-    whole[rep] = total.astype(bf16)
-
-    def all_copy(j):
-        return pltpu.make_async_remote_copy(
-            src_ref=whole.at[rep],
-            dst_ref=whole.at[rep],
-            send_sem=all_send.at[j],
-            recv_sem=all_recv.at[rep],
-            device_id=dev(y, z, (rep + j) % 8),
-            device_id_type=MESH,
-        )
-
-    def send_all(j, carry):
-        all_copy(j).start()
-        return carry
-
-    lax.fori_loop(1, 8, send_all, 0)
+    lax.fori_loop(20, 28, add_pair, 0)
 
     def zb_copy(k):
         return pltpu.make_async_remote_copy(
@@ -666,7 +630,7 @@
             dst_ref=strip.at[:, cols(z, VCOLS)],
             send_sem=zb_send.at[k],
             recv_sem=zb_recv.at[z],
-            device_id=dev(y, (z + k) % 16, rep),
+            device_id=dev(y, (z + k) & 15, rep),
             device_id_type=MESH,
         )
 
@@ -678,7 +642,7 @@
                 dst_ref=z_in.at[k],
                 send_sem=z_send.at[k],
                 recv_sem=z_recv.at[k],
-                device_id=dev(y, (z + 16 - k) % 16, rep),
+                device_id=dev(y, (z + 16 - k) & 15, rep),
                 device_id_type=MESH,
             ).wait_recv()
             return carry
@@ -695,8 +659,37 @@
 
         lax.fori_loop(1, 16, zb_start, 0)
 
+    lax.fori_loop(28, 32, add_pair, 0)
+
+
+    def sum_copy(j):
+        return pltpu.make_async_remote_copy(
+            src_ref=part_out.at[j],
+            dst_ref=part_in.at[group],
+            send_sem=part_send.at[j],
+            recv_sem=part_recv.at[group],
+            device_id=dev(y, owner_z, j),
+            device_id_type=MESH,
+        )
+
+    def send_sum(j, carry):
+        part_out[j] = acc[pl.ds(pl.multiple_of(j * PART, PART), PART), :].astype(bf16)
+        other = jnp.logical_or(owner_z != z, j != rep)
+
+        @pl.when(other)
+        def _():
+            sum_copy(j).start()
+
+        @pl.when(jnp.logical_not(other))
+        def _():
+            part_in[group] = part_out[j]
+
+        return carry
+
+    lax.fori_loop(0, 8, send_sum, 0)
+
     def zb_wait(k, carry):
-        other = (z + 16 - k) % 16
+        other = (z + 16 - k) & 15
 
         @pl.when(other < VCHUNKS)
         def _():
@@ -721,14 +714,60 @@
             dst_ref=total_ref.at[band(y), :],
             send_sem=yb_send.at[k],
             recv_sem=yb_recv.at[k],
-            device_id=dev((y + k) % 4, z, rep),
+            device_id=dev((y + k) & 3, z, rep),
             device_id_type=MESH,
         )
         copy.start()
         yb_copies.append(copy)
 
+    def drain(i):
+        m = peer(i, y, z, rep)
+        ask_copy(m).wait_send()
+        reply_copy(m).wait_send()
+        out_copy(m).wait_send()
+
+    others(GROUP, drain)
+
+    def await_sum(j, carry):
+        sz, srep = holder(j)
+
+        @pl.when(is_other((sz, srep)))
+        def _():
+            pltpu.make_async_remote_copy(
+                src_ref=part_out.at[0],
+                dst_ref=part_in.at[sz >> 1],
+                send_sem=part_send.at[0],
+                recv_sem=part_recv.at[sz >> 1],
+                device_id=dev(y, sz, srep),
+                device_id_type=MESH,
+            ).wait_recv()
+
+        return carry
+
+    lax.fori_loop(0, 8, await_sum, 0)
+    total = part_in[0].astype(f32)
+    for g in range(1, 8):
+        total = total + part_in[g].astype(f32)
+    whole[rep] = total.astype(bf16)
+
+    def all_copy(j):
+        return pltpu.make_async_remote_copy(
+            src_ref=whole.at[rep],
+            dst_ref=whole.at[rep],
+            send_sem=all_send.at[j],
+            recv_sem=all_recv.at[rep],
+            device_id=dev(y, z, (rep + j) & 7),
+            device_id_type=MESH,
+        )
+
+    def send_all(j, carry):
+        all_copy(j).start()
+        return carry
+
+    lax.fori_loop(1, 8, send_all, 0)
+
     def await_all(j, carry):
-        other = (rep + 8 - j) % 8
+        other = (rep + 8 - j) & 7
         pltpu.make_async_remote_copy(
             src_ref=whole.at[other],
             dst_ref=whole.at[other],
@@ -742,29 +781,21 @@
     lax.fori_loop(1, 8, await_all, 0)
     grad_ref[...] = whole[...].astype(f32)
     for k in (2, 1, 3):
-        came = band((y + 4 - k) % 4)
+        came = band((y + 4 - k) & 3)
         pltpu.make_async_remote_copy(
             src_ref=total_ref.at[came, :],
             dst_ref=total_ref.at[came, :],
             send_sem=yb_send.at[k],
             recv_sem=yb_recv.at[k],
-            device_id=dev((y + 4 - k) % 4, z, rep),
+            device_id=dev((y + 4 - k) & 3, z, rep),
             device_id_type=MESH,
         ).wait_recv()
 
     for copy in w_copies + wc_copies + core_copies + x_copies + y_copies + yb_copies:
         copy.wait_send()
 
-    def drain(i):
-        m = peer(i, y, z, rep)
-        ask_copy(m).wait_send()
-        reply_copy(m).wait_send()
-        out_copy(m).wait_send()
-
-    others(GROUP, drain)
-
     def drain_parts(j, carry):
-        @pl.when(jnp.logical_or(holder(j) != z, home != rep))
+        @pl.when(is_other(holder(j)))
         def _():
             part_copy(j).wait_send()
 
@@ -783,7 +814,7 @@
     lax.fori_loop(1, 8, drain_all, 0)
 
     def drain_z(k, carry):
-        @pl.when((z + k) % 16 < VCHUNKS)
+        @pl.when((z + k) & 15 < VCHUNKS)
         def _():
             z_copy(k).wait_send()
 
@@ -798,6 +829,10 @@
 
 def vmem():
     return pl.BlockSpec(memory_space=pltpu.VMEM)
+
+
+def hbm():
+    return pl.BlockSpec(memory_space=pl.ANY)
 
 
 def dma(n):
@@ -811,9 +846,13 @@
             jax.ShapeDtypeStruct((8, PART, ROWS), f32),
             jax.ShapeDtypeStruct((V_ROWS, CROSS), f32),
         ),
-        in_specs=[vmem()] * 11,
+        in_specs=[
+            vmem(), vmem(), hbm(), vmem(), vmem(), hbm(), hbm(), vmem(), vmem(), vmem(), vmem(),
+        ],
         out_specs=(vmem(), vmem()),
         scratch_shapes=[
+            pltpu.VMEM((NHOT, E, E), bf16),
+            pltpu.VMEM((V_ROWS, CROSS), bf16),
             pltpu.VMEM((8, PART, ROWS), bf16),
             pltpu.VMEM((GROUP, E, SLOTS), bf16),
             pltpu.VMEM((GROUP, E, SLOTS), bf16),
@@ -846,7 +885,7 @@
             pltpu.VMEM((8, PADDED), f32),
             pltpu.VMEM((16, 8, VCOLS), f32),
             pltpu.VMEM((8, PADDED), f32),
-            dma(8), dma(8), dma(GROUP), dma(GROUP), dma(GROUP), dma(GROUP), dma(3),
+            dma(8), dma(8), dma(GROUP), dma(GROUP), dma(GROUP), dma(GROUP), dma(4),
             dma(8), dma(8), dma(8), dma(8),
             dma(GROUP), dma(GROUP), dma(8), dma(8), dma(8), dma(8),
             dma(4), dma(4), dma(4), dma(4), dma(4), dma(4),
@@ -877,8 +916,8 @@
     turned = cold_rows.reshape(NCOLD, ROWS, E).transpose(0, 2, 1).reshape(8, PART, ROWS)
     part = lax.dynamic_index_in_dim(turned, rep, 0, keepdims=False).astype(bf16)
     grad_rows, grad_mine = step_call(
-        cold_owner.T, cold_row.T, part, bottom, hot_ids, hot_tables, u_weight,
-        v_weight.astype(bf16), cross_bias[None, :], head[None, :], labels[:, None],
+        cold_owner.T, cold_row.T, part, bottom, hot_ids.T, hot_tables, u_weight, v_weight,
+        cross_bias.reshape(CROSS // E, E), head.reshape(CROSS // E, E), labels.reshape(2, E),
     )
     grad_rows = grad_rows.reshape(NCOLD, E, ROWS).transpose(0, 2, 1).reshape(NCOLD * ROWS, E)
     new_cold_acc = cold_acc + jnp.mean(grad_rows * grad_rows, axis=1)

time: 228 us -> 199 us (0.87)
  the two profiles are of different devices: /device:TPU:2 before, /device:TPU:29 now
where the time goes in v3:
time: 199 us; the launch traced here: 198 us
  Pallas kernels  191 us (96%)
  other arithmetic  4.11 us (2%)
  local copies, waits for them, and re-layouts  2.96 us (1%)
    pallas_call x1, Pallas kernels, step_call(): pl.pallas_call(step_kernel, out_shape=(jax.ShapeDtypeStruct((8, PART, ROW...  191 us

profile of v3, /device:TPU:29, one launch (start us, length us, event | category | flops | bytes accessed | tf_op | source)
XLA Modules:
  0.0 198.4 jit_solution(13671446822570633886)
XLA Ops:
  0.6 1.3 copy.16
  1.9 0.6 fusion.1.part_ref
  2.6 0.0 copy-start.5
  2.6 0.0 copy-start.2
  2.6 190.6 %shard_map.148 = (f32[8,96,256]{2,1,0:T(8,128)}, f32[32,3456]{1,0:T(8,128)}) custom-call(s32[12,256]{1,0:T(8,128)} %bitcast.25, s32[12,256]{1,0:T(8,128)} %bitcast.26, bf16[96,256]{1,0:T(8,128)(2,1)} %fusion.1.part_ref, bf16[256,128]{1,0:T(8,128)(2,1)} %bottom_ref.1, s32[20,256]{1,0:T(8,128)} %bitcast.24, bf16[20,128,128]{2,1,0:T(8,128)(2,1)} %hot_hbm.1, ...), custom_call_target="tpu_custom_call" | custom-call | tf_op jit(solution)/shard_map/pallas_call | solution.py:843
  193.2 0.0 copy-start.1
  193.2 0.0 copy-start.3
  193.2 1.2 multiply_reduce_fusion
  194.5 0.0 copy-done.5
  194.5 0.0 copy-done.2
  194.5 0.0 copy-done.1
  194.5 0.9 divide_subtract_fusion
  195.4 0.0 copy-done.3
  195.4 0.2 broadcast_multiply_fusion
  195.6 0.3 copy.17
  195.8 0.0 copy-start
  195.8 0.1 reduce_sum.18
  195.9 0.0 copy-start.4
  195.9 0.7 copy-done.4
  196.7 0.6 sqrt_add_fusion
  197.3 0.0 copy-done
  197.3 1.2 fusion
  (3 shorter events, 0.0 us)
Async XLA Ops:
  2.6 191.9 %copy-start.5 = (f32[32]{0:T(128)S(1)}, f32[32]{0:T(128)}, u32[]{:S(2)}) copy-start(f32[32]{0:T(128)} %param.22) | copy-start | bytes 388
  2.6 191.9 %copy-start.2 = (f32[32,3456]{1,0:T(8,128)S(1)}, f32[32,3456]{1,0:T(8,128)}, u32[]{:S(2)}) copy-start(f32[32,3456]{1,0:T(8,128)} %v_wide.1) | copy-start | bytes 1327108
  193.2 1.3 copy-start.1
  193.2 2.2 %copy-start.3 = (f32[8,96,256]{2,1,0:T(8,128)S(1)}, f32[8,96,256]{2,1,0:T(8,128)}, u32[]{:S(2)}) copy-start(f32[8,96,256]{2,1,0:T(8,128)} %get-tuple-element.5) | copy-start | bytes 2359300
  195.8 1.5 copy-start
  195.9 0.8 copy-start.4

commit v4 on v3

--- a/solution.py
+++ b/solution.py
@@ -17,16 +17,18 @@
 GROUP = 64
 ITSELF = 40
 PAIR_SELF = ITSELF // 2
+V_START = 24
 WIDE = NCOLD * E
 PART = WIDE // 8
 CROSS = 3456
 PADDED = 3584
 COLS = 384
 U_ROWS = 432
+U_PIECE = 112
+V_PIECE = 896
 V_ROWS = 32
 RANK = 256
 VCHUNKS = 14
-VCOLS = 256
 MESH = pl.DeviceIdType.MESH
 
 row_rate = 0.1
@@ -126,9 +128,9 @@
     hot_ref, v_ref, held, replies, back, ask, asked, pos, tab, rows, picks, pooled,
     u_full, v_full, first, mixed, low_t, dlow, dpool, grads,
     arrived, out, acc, part_out, part_in, whole,
-    core_in, pair, x_in, mine, y_in, column, z_in, strip,
+    core_in, pair, y_in, band, x_in, mine, z_in, strip, summed,
     held_send, held_recv, ask_send, ask_recv, rep_send, rep_recv, own_sem,
-    w_send, w_recv, wc_send, wc_recv,
+    w_send, w_recv, wy_send, wy_recv, wc_send, wc_recv,
     out_send, out_recv, part_send, part_recv, all_send, all_recv,
     core_send, core_recv, x_send, x_recv, y_send, y_recv, z_send, z_recv, zb_send, zb_recv, yb_send, yb_recv,
 ):
@@ -231,11 +233,66 @@
             for i, (src, dst) in enumerate([(src_u, u_at(r)), (src_v, v_at(r))])
         ]
 
-    w_copies = []
+    def quarter(q, act):
+        @pl.when(q < 3)
+        def _():
+            act(U_PIECE, V_PIECE)
+
+        @pl.when(q == 3)
+        def _():
+            act(U_ROWS - 3 * U_PIECE, CROSS - 3 * V_PIECE)
+
+    def u_piece(ref, base, q, n):
+        return ref.at[pl.ds(pl.multiple_of(base + q * U_PIECE, 16), n), :]
+
+    def v_piece(ref, base, q, n):
+        at = pl.ds(pl.multiple_of(q * V_PIECE, V_PIECE), n)
+        return ref.at[pl.ds(pl.multiple_of(base, 16), V_ROWS), at]
+
+    def x_weights(k, r, to, act):
+        def run(u_n, v_n):
+            pairs = [
+                (u_piece(u_ref, 0, y, u_n), u_piece(u_full, r * U_ROWS, y, u_n)),
+                (v_piece(v_ref, 0, y, v_n), v_piece(v_full, r * V_ROWS, y, v_n)),
+            ]
+            for i, (src, dst) in enumerate(pairs):
+                act(
+                    pltpu.make_async_remote_copy(
+                        src_ref=src,
+                        dst_ref=dst,
+                        send_sem=w_send.at[2 * k + i],
+                        recv_sem=w_recv.at[2 * k + i],
+                        device_id=dev(y, z, to),
+                        device_id_type=MESH,
+                    )
+                )
+
+        quarter(y, run)
+
+    def y_weights(k, n, q, to, act):
+        r = ((x + 4 - k) & 3) * 2 + c
+
+        def run(u_n, v_n):
+            for i, ref in enumerate(
+                [u_piece(u_full, r * U_ROWS, q, u_n), v_piece(v_full, r * V_ROWS, q, v_n)]
+            ):
+                sem = (k * 4 + n) * 2 + i
+                act(
+                    pltpu.make_async_remote_copy(
+                        src_ref=ref,
+                        dst_ref=ref,
+                        send_sem=wy_send.at[sem],
+                        recv_sem=wy_recv.at[sem],
+                        device_id=dev(to, z, rep),
+                        device_id_type=MESH,
+                    )
+                )
+
+        quarter(q, run)
+
     for k in (2, 1, 3):
-        to = ((x + k) & 3) * 2 + c
-        w_copies += weight_copies(u_ref, v_ref, rep, w_send, w_recv, k, y, z, to)
-    w_copies += weight_copies(u_ref, v_ref, rep, w_send, w_recv, 0, y, z, sibling)
+        x_weights(k, rep, ((x + k) & 3) * 2 + c, lambda copy: copy.start())
+    w_copies = weight_copies(u_ref, v_ref, rep, w_send, w_recv, 0, y, z, sibling)
     for copy in w_copies:
         copy.start()
     own_u = pltpu.make_async_copy(u_ref, u_at(rep), own_sem.at[1])
@@ -294,15 +351,11 @@
         at = E + WIDE + j * E
         first[:, at : at + E] = jnp.dot(one, hot_ref[j], preferred_element_type=f32).astype(bf16)
 
-    wc_copies = []
     for k in (1, 3, 2):
         came = ((x + 4 - k) & 3) * 2 + c
-        for copy in weight_copies(u_at(came), v_at(came), came, w_send, w_recv, k, y, z, came):
-            copy.wait_recv()
-        forward = weight_copies(u_at(came), v_at(came), came, wc_send, wc_recv, k, y, z, sibling)
-        for copy in forward:
-            copy.start()
-        wc_copies += forward
+        x_weights(k, came, came, lambda copy: copy.wait_recv())
+        for n in (2, 1, 3):
+            y_weights(k, n, y, (y + n) & 3, lambda copy: copy.start())
 
     def await_part(j, carry):
         sz, srep = source(j)
@@ -378,6 +431,49 @@
         return carry
 
     lax.fori_loop(0, GROUP // 2, reply_pair, 0)
+
+    wc_copies = []
+    for k in (1, 3, 2):
+        for n in (1, 3, 2):
+            came = (y + 4 - n) & 3
+            y_weights(k, n, came, came, lambda copy: copy.wait_recv())
+        came = ((x + 4 - k) & 3) * 2 + c
+        forward = weight_copies(u_at(came), v_at(came), came, wc_send, wc_recv, k, y, z, sibling)
+        for copy in forward:
+            copy.start()
+        wc_copies += forward
+
+    pooled[...] = jnp.zeros((WIDE, B), f32)
+
+    def await_reply(m):
+        pltpu.make_async_remote_copy(
+            src_ref=back.at[m],
+            dst_ref=replies.at[m],
+            send_sem=rep_send.at[m],
+            recv_sem=rep_recv.at[m],
+            device_id=member_dev(m, z),
+            device_id_type=MESH,
+        ).wait_recv()
+
+    def pool_pair(p, carry):
+        a, b = peer(2 * p, y, z, rep), peer(2 * p + 1, y, z, rep)
+
+        @pl.when(p != PAIR_SELF)
+        def _():
+            await_reply(a)
+
+        await_reply(b)
+        got_a = jnp.dot(replies[a], picks[a], preferred_element_type=f32)
+        got_b = jnp.dot(replies[b], picks[b], preferred_element_type=f32)
+        tab_a, tab_b = tab[pl.ds(a, 1), :], tab[pl.ds(b, 1), :]
+        for t in range(NCOLD):
+            more = jnp.where(tab_a == float(t), got_a, 0.0) + jnp.where(
+                tab_b == float(t), got_b, 0.0
+            )
+            pooled[t * E : (t + 1) * E, :] += more
+        return carry
+
+    lax.fori_loop(0, 20, pool_pair, 0)
 
     for k in range(4):
         came = ((x + 4 - k) & 3) * 2 + other_c
@@ -390,37 +486,7 @@
     low = jnp.dot(first[:, 0:E], u_full[0:E, :], preferred_element_type=f32)
     low = low + jnp.dot(first[:, hot_at:], u_full[hot_at:, :], preferred_element_type=f32)
 
-    pooled[...] = jnp.zeros((WIDE, B), f32)
-
-    def await_reply(m):
-        pltpu.make_async_remote_copy(
-            src_ref=back.at[m],
-            dst_ref=replies.at[m],
-            send_sem=rep_send.at[m],
-            recv_sem=rep_recv.at[m],
-            device_id=member_dev(m, z),
-            device_id_type=MESH,
-        ).wait_recv()
-
-    def pool_pair(p, carry):
-        a, b = peer(2 * p, y, z, rep), peer(2 * p + 1, y, z, rep)
-
-        @pl.when(p != PAIR_SELF)
-        def _():
-            await_reply(a)
-
-        await_reply(b)
-        got_a = jnp.dot(replies[a], picks[a], preferred_element_type=f32)
-        got_b = jnp.dot(replies[b], picks[b], preferred_element_type=f32)
-        tab_a, tab_b = tab[pl.ds(a, 1), :], tab[pl.ds(b, 1), :]
-        for t in range(NCOLD):
-            more = jnp.where(tab_a == float(t), got_a, 0.0) + jnp.where(
-                tab_b == float(t), got_b, 0.0
-            )
-            pooled[t * E : (t + 1) * E, :] += more
-        return carry
-
-    lax.fori_loop(0, GROUP // 2, pool_pair, 0)
+    lax.fori_loop(20, 32, pool_pair, 0)
     for t in range(NCOLD):
         first[:, E + t * E : E + (t + 1) * E] = pooled[t * E : (t + 1) * E, :].T.astype(bf16)
 
@@ -452,6 +518,7 @@
     dlogit = jax.nn.sigmoid(logit) - label[:, 0:1]
 
     dlow[...] = jnp.zeros((B, RANK), f32)
+    grads[:, CROSS:] = jnp.zeros((RANK, PADDED - CROSS), bf16)
 
     def backward_cols(i, carry):
         at = cols(i, COLS)
@@ -519,28 +586,11 @@
         out_copy(b).start()
         return carry
 
-    lax.fori_loop(0, 16, pack_pair, 0)
+    lax.fori_loop(0, 32, pack_pair, 0)
 
     for k in range(4):
         core_copies[k].wait_recv()
-        pair[k] = (
-            grads[v_rows(2 * k + c), :].astype(f32) + core_in[k].astype(f32)
-        ).astype(bf16)
-    x_copies = []
-    for k in (2, 1, 3):
-        to = (x + k) & 3
-        copy = pltpu.make_async_remote_copy(
-            src_ref=pair.at[to],
-            dst_ref=x_in.at[k],
-            send_sem=x_send.at[k],
-            recv_sem=x_recv.at[k],
-            device_id=dev(y, z, to * 2 + c),
-            device_id_type=MESH,
-        )
-        copy.start()
-        x_copies.append(copy)
-
-    lax.fori_loop(16, 32, pack_pair, 0)
+        pair[k] = (grads[v_rows(2 * k + c), :].astype(f32) + core_in[k].astype(f32)).astype(bf16)
 
 
     acc[...] = jnp.zeros((WIDE, ROWS), f32)
@@ -572,22 +622,16 @@
         acc[...] += lax.dot_general(lhs, rows_of(code), NT, preferred_element_type=f32)
         return carry
 
-    lax.fori_loop(0, 12, add_pair, 0)
-
-    for copy in x_copies:
-        copy.wait_recv()
-    mine[...] = (
-        pair[x].astype(f32) + x_in[1].astype(f32) + x_in[2].astype(f32) + x_in[3].astype(f32)
-    )
-
-    def band(j):
-        return pl.ds(pl.multiple_of(j * 8, 8), 8)
+    lax.fori_loop(0, V_START, add_pair, 0)
+
+    def piece(j):
+        return pl.ds(pl.multiple_of(j * V_PIECE, V_PIECE), V_PIECE)
 
     y_copies = []
     for k in (2, 1, 3):
         to = (y + k) & 3
         copy = pltpu.make_async_remote_copy(
-            src_ref=mine.at[band(to), :],
+            src_ref=pair.at[:, :, piece(to)],
             dst_ref=y_in.at[k],
             send_sem=y_send.at[k],
             recv_sem=y_recv.at[k],
@@ -596,16 +640,70 @@
         )
         copy.start()
         y_copies.append(copy)
-    lax.fori_loop(12, 20, add_pair, 0)
+    lax.fori_loop(V_START, 32, add_pair, 0)
+
+
+    def sum_copy(j):
+        return pltpu.make_async_remote_copy(
+            src_ref=part_out.at[j],
+            dst_ref=part_in.at[group],
+            send_sem=part_send.at[j],
+            recv_sem=part_recv.at[group],
+            device_id=dev(y, owner_z, j),
+            device_id_type=MESH,
+        )
+
+    def send_sum(j, carry):
+        part_out[j] = acc[pl.ds(pl.multiple_of(j * PART, PART), PART), :].astype(bf16)
+        other = jnp.logical_or(owner_z != z, j != rep)
+
+        @pl.when(other)
+        def _():
+            sum_copy(j).start()
+
+        @pl.when(jnp.logical_not(other))
+        def _():
+            part_in[group] = part_out[j]
+
+        return carry
+
+    lax.fori_loop(0, 8, send_sum, 0)
+
     for copy in y_copies:
         copy.wait_recv()
-    column[:, CROSS:] = jnp.zeros((8, PADDED - CROSS), f32)
-    column[:, :CROSS] = mine[band(y), :] + y_in[1] + y_in[2] + y_in[3]
+    for k in range(4):
+        band[k] = (
+            pair[k, :, piece(y)].astype(f32)
+            + y_in[1, k].astype(f32)
+            + y_in[2, k].astype(f32)
+            + y_in[3, k].astype(f32)
+        )
+    x_copies = []
+    for k in (2, 1, 3):
+        to = (x + k) & 3
+        copy = pltpu.make_async_remote_copy(
+            src_ref=band.at[to],
+            dst_ref=x_in.at[k],
+            send_sem=x_send.at[k],
+            recv_sem=x_recv.at[k],
+            device_id=dev(y, z, to * 2 + c),
+            device_id_type=MESH,
+        )
+        copy.start()
+        x_copies.append(copy)
+    for copy in x_copies:
+        copy.wait_recv()
+    mine[...] = band[x] + x_in[1] + x_in[2] + x_in[3]
+
+    def block(ref, j):
+        return ref.at[
+            pl.ds(pl.multiple_of((j & 1) * 16, 16), 16), pl.ds(pl.multiple_of((j >> 1) * E, E), E)
+        ]
 
     def z_copy(k):
         to = (z + k) & 15
         return pltpu.make_async_remote_copy(
-            src_ref=column.at[:, cols(to, VCOLS)],
+            src_ref=block(mine, to),
             dst_ref=z_in.at[k],
             send_sem=z_send.at[k],
             recv_sem=z_recv.at[k],
@@ -622,12 +720,10 @@
 
     lax.fori_loop(1, 16, z_start, 0)
 
-    lax.fori_loop(20, 28, add_pair, 0)
-
     def zb_copy(k):
         return pltpu.make_async_remote_copy(
-            src_ref=strip.at[:, cols(z, VCOLS)],
-            dst_ref=strip.at[:, cols(z, VCOLS)],
+            src_ref=block(strip, z),
+            dst_ref=block(strip, z),
             send_sem=zb_send.at[k],
             recv_sem=zb_recv.at[z],
             device_id=dev(y, (z + k) & 15, rep),
@@ -648,77 +744,16 @@
             return carry
 
         lax.fori_loop(1, 16, z_wait, 0)
-        summed = column[:, cols(z, VCOLS)]
+        got = block(mine, z)[...]
         for k in range(1, 16):
-            summed = summed + z_in[k]
-        strip[:, cols(z, VCOLS)] = summed
+            got = got + z_in[k]
+        block(strip, z)[...] = got
 
         def zb_start(k, carry):
             zb_copy(k).start()
             return carry
 
         lax.fori_loop(1, 16, zb_start, 0)
-
-    lax.fori_loop(28, 32, add_pair, 0)
-
-
-    def sum_copy(j):
-        return pltpu.make_async_remote_copy(
-            src_ref=part_out.at[j],
-            dst_ref=part_in.at[group],
-            send_sem=part_send.at[j],
-            recv_sem=part_recv.at[group],
-            device_id=dev(y, owner_z, j),
-            device_id_type=MESH,
-        )
-
-    def send_sum(j, carry):
-        part_out[j] = acc[pl.ds(pl.multiple_of(j * PART, PART), PART), :].astype(bf16)
-        other = jnp.logical_or(owner_z != z, j != rep)
-
-        @pl.when(other)
-        def _():
-            sum_copy(j).start()
-
-        @pl.when(jnp.logical_not(other))
-        def _():
-            part_in[group] = part_out[j]
-
-        return carry
-
-    lax.fori_loop(0, 8, send_sum, 0)
-
-    def zb_wait(k, carry):
-        other = (z + 16 - k) & 15
-
-        @pl.when(other < VCHUNKS)
-        def _():
-            pltpu.make_async_remote_copy(
-                src_ref=strip.at[:, cols(other, VCOLS)],
-                dst_ref=strip.at[:, cols(other, VCOLS)],
-                send_sem=zb_send.at[k],
-                recv_sem=zb_recv.at[other],
-                device_id=dev(y, other, rep),
-                device_id_type=MESH,
-            ).wait_recv()
-
-        return carry
-
-    lax.fori_loop(1, 16, zb_wait, 0)
-
-    total_ref[band(y), :] = strip[:, :CROSS]
-    yb_copies = []
-    for k in (2, 1, 3):
-        copy = pltpu.make_async_remote_copy(
-            src_ref=total_ref.at[band(y), :],
-            dst_ref=total_ref.at[band(y), :],
-            send_sem=yb_send.at[k],
-            recv_sem=yb_recv.at[k],
-            device_id=dev((y + k) & 3, z, rep),
-            device_id_type=MESH,
-        )
-        copy.start()
-        yb_copies.append(copy)
 
     def drain(i):
         m = peer(i, y, z, rep)
@@ -766,6 +801,37 @@
 
     lax.fori_loop(1, 8, send_all, 0)
 
+    def zb_wait(k, carry):
+        other = (z + 16 - k) & 15
+
+        @pl.when(other < VCHUNKS)
+        def _():
+            pltpu.make_async_remote_copy(
+                src_ref=block(strip, other),
+                dst_ref=block(strip, other),
+                send_sem=zb_send.at[k],
+                recv_sem=zb_recv.at[other],
+                device_id=dev(y, other, rep),
+                device_id_type=MESH,
+            ).wait_recv()
+
+        return carry
+
+    lax.fori_loop(1, 16, zb_wait, 0)
+    summed[:, piece(y)] = strip[...]
+    yb_copies = []
+    for k in (2, 1, 3):
+        copy = pltpu.make_async_remote_copy(
+            src_ref=summed.at[:, piece(y)],
+            dst_ref=summed.at[:, piece(y)],
+            send_sem=yb_send.at[k],
+            recv_sem=yb_recv.at[k],
+            device_id=dev((y + k) & 3, z, rep),
+            device_id_type=MESH,
+        )
+        copy.start()
+        yb_copies.append(copy)
+
     def await_all(j, carry):
         other = (rep + 8 - j) & 7
         pltpu.make_async_remote_copy(
@@ -780,17 +846,22 @@
 
     lax.fori_loop(1, 8, await_all, 0)
     grad_ref[...] = whole[...].astype(f32)
-    for k in (2, 1, 3):
-        came = band((y + 4 - k) & 3)
+    for k in (1, 3, 2):
+        came = piece((y + 4 - k) & 3)
         pltpu.make_async_remote_copy(
-            src_ref=total_ref.at[came, :],
-            dst_ref=total_ref.at[came, :],
+            src_ref=summed.at[:, came],
+            dst_ref=summed.at[:, came],
             send_sem=yb_send.at[k],
             recv_sem=yb_recv.at[k],
             device_id=dev((y + 4 - k) & 3, z, rep),
             device_id_type=MESH,
         ).wait_recv()
-
+    total_ref[...] = summed[:, :CROSS]
+
+    for k in (1, 2, 3):
+        x_weights(k, rep, ((x + k) & 3) * 2 + c, lambda copy: copy.wait_send())
+        for n in (1, 2, 3):
+            y_weights(k, n, y, (y + n) & 3, lambda copy: copy.wait_send())
     for copy in w_copies + wc_copies + core_copies + x_copies + y_copies + yb_copies:
         copy.wait_send()
 
@@ -870,23 +941,24 @@
             pltpu.VMEM((RANK, B), bf16),
             pltpu.VMEM((B, RANK), f32),
             pltpu.VMEM((WIDE, B), f32),
-            pltpu.VMEM((RANK, CROSS), bf16),
+            pltpu.VMEM((RANK, PADDED), bf16),
             pltpu.VMEM((GROUP, E, SLOTS), bf16),
             pltpu.VMEM((GROUP, E, SLOTS), bf16),
             pltpu.VMEM((WIDE, ROWS), f32),
             pltpu.VMEM((8, PART, ROWS), bf16),
             pltpu.VMEM((8, PART, ROWS), bf16),
             pltpu.VMEM((8, PART, ROWS), bf16),
-            pltpu.VMEM((4, V_ROWS, CROSS), bf16),
-            pltpu.VMEM((4, V_ROWS, CROSS), bf16),
-            pltpu.VMEM((4, V_ROWS, CROSS), bf16),
-            pltpu.VMEM((V_ROWS, CROSS), f32),
-            pltpu.VMEM((4, 8, CROSS), f32),
-            pltpu.VMEM((8, PADDED), f32),
-            pltpu.VMEM((16, 8, VCOLS), f32),
-            pltpu.VMEM((8, PADDED), f32),
+            pltpu.VMEM((4, V_ROWS, PADDED), bf16),
+            pltpu.VMEM((4, V_ROWS, PADDED), bf16),
+            pltpu.VMEM((4, 4, V_ROWS, V_PIECE), bf16),
+            pltpu.VMEM((4, V_ROWS, V_PIECE), f32),
+            pltpu.VMEM((4, V_ROWS, V_PIECE), f32),
+            pltpu.VMEM((V_ROWS, V_PIECE), f32),
+            pltpu.VMEM((16, 16, E), f32),
+            pltpu.VMEM((V_ROWS, V_PIECE), f32),
+            pltpu.VMEM((V_ROWS, PADDED), f32),
             dma(8), dma(8), dma(GROUP), dma(GROUP), dma(GROUP), dma(GROUP), dma(4),
-            dma(8), dma(8), dma(8), dma(8),
+            dma(8), dma(8), dma(32), dma(32), dma(8), dma(8),
             dma(GROUP), dma(GROUP), dma(8), dma(8), dma(8), dma(8),
             dma(4), dma(4), dma(4), dma(4), dma(4), dma(4),
             dma(16), dma(16), dma(16), dma(16), dma(4), dma(4),

time: 199 us -> 180 us (0.905)
  the two profiles are of different devices: /device:TPU:29 before, /device:TPU:2 now
where the time goes in v4:
time: 180 us
  Pallas kernels  172 us (96%)
  other arithmetic  4.11 us (2%)
  local copies, waits for them, and re-layouts  2.96 us (2%)
    pallas_call x1, Pallas kernels, step_call(): pl.pallas_call(step_kernel, out_shape=(jax.ShapeDtypeStruct((8, PART, ROW...  172 us

profile of v4, /device:TPU:2, one launch (start us, length us, event | category | flops | bytes accessed | tf_op | source)
XLA Modules:
  0.0 179.7 jit_solution(9649238722760994371)
XLA Ops:
  0.6 1.3 copy.16
  1.9 0.6 fusion.1.part_ref
  2.6 0.0 copy-start.5
  2.6 0.0 copy-start.2
  2.6 171.9 %shard_map.148 = (f32[8,96,256]{2,1,0:T(8,128)}, f32[32,3456]{1,0:T(8,128)}) custom-call(s32[12,256]{1,0:T(8,128)} %bitcast.25, s32[12,256]{1,0:T(8,128)} %bitcast.26, bf16[96,256]{1,0:T(8,128)(2,1)} %fusion.1.part_ref, bf16[256,128]{1,0:T(8,128)(2,1)} %bottom_ref.1, s32[20,256]{1,0:T(8,128)} %bitcast.24, bf16[20,128,128]{2,1,0:T(8,128)(2,1)} %hot_hbm.1, ...), custom_call_target="tpu_custom_call" | custom-call | tf_op jit(solution)/shard_map/pallas_call | solution.py:914
  174.5 0.0 copy-start.1
  174.5 0.0 copy-start.3
  174.5 1.2 multiply_reduce_fusion
  175.7 0.0 copy-done.5
  175.8 0.0 copy-done.2
  175.8 0.0 copy-done.1
  175.8 0.9 divide_subtract_fusion
  176.7 0.0 copy-done.3
  176.7 0.2 broadcast_multiply_fusion
  176.8 0.3 copy.17
  177.1 0.0 copy-start
  177.1 0.1 reduce_sum.18
  177.2 0.0 copy-start.4
  177.2 0.7 copy-done.4
  177.9 0.6 sqrt_add_fusion
  178.5 0.0 copy-done
  178.5 1.2 fusion
  (3 shorter events, 0.0 us)
Async XLA Ops:
  2.6 173.2 %copy-start.5 = (f32[32]{0:T(128)S(1)}, f32[32]{0:T(128)}, u32[]{:S(2)}) copy-start(f32[32]{0:T(128)} %param.22) | copy-start | bytes 388
  2.6 173.2 %copy-start.2 = (f32[32,3456]{1,0:T(8,128)S(1)}, f32[32,3456]{1,0:T(8,128)}, u32[]{:S(2)}) copy-start(f32[32,3456]{1,0:T(8,128)} %v_wide.1) | copy-start | bytes 1327108
  174.5 1.3 copy-start.1
  174.5 2.2 %copy-start.3 = (f32[8,96,256]{2,1,0:T(8,128)S(1)}, f32[8,96,256]{2,1,0:T(8,128)}, u32[]{:S(2)}) copy-start(f32[8,96,256]{2,1,0:T(8,128)} %get-tuple-element.5) | copy-start | bytes 2359300
  177.1 1.5 copy-start
  177.2 0.8 copy-start.4

commit v5 on v4

--- a/solution.py
+++ b/solution.py
@@ -15,7 +15,7 @@
 ROWS = 256
 SLOTS = 128
 GROUP = 64
-ITSELF = 40
+ITSELF = 8
 PAIR_SELF = ITSELF // 2
 V_START = 24
 WIDE = NCOLD * E
@@ -72,14 +72,14 @@
     px = ((rep >> 1) + 2 + (i >> 2)) & 3
     pc = (rep + (i >> 1)) & 1
     pz = (z - (z & 1)) + ((z + i) & 1)
-    return member_of((y + 2 + (i >> 4)) & 3, pz, px * 2 + pc)
+    return (y + 2 + (i >> 4) + (i >> 2)) & 3, pz, px * 2 + pc
 
 
 def peer_back(i, y, z, rep):
     px = ((rep >> 1) + 6 - ((i >> 2) & 3)) & 3
     pc = (rep + (i >> 1)) & 1
     pz = (z - (z & 1)) + ((z + i) & 1)
-    return member_of((y + 6 - (i >> 4)) & 3, pz, px * 2 + pc)
+    return (y + 6 - (((i >> 4) + (i >> 2)) & 3)) & 3, pz, px * 2 + pc
 
 
 def tables(owner_ref, row_ref, pos, tab, rows):
@@ -152,9 +152,7 @@
         pl.semaphore_signal(bar, inc=1, device_id=dev(y_, z_, rep_), device_id_type=MESH)
 
     def greet_member(i):
-        pl.semaphore_signal(
-            bar, inc=1, device_id=member_dev(peer(i, y, z, rep), z), device_id_type=MESH
-        )
+        signal(*peer(i, y, z, rep))
 
     others(GROUP, greet_member)
 
@@ -302,18 +300,20 @@
 
     lines16 = lax.broadcasted_iota(i32, (16, B), 0)
 
-    def ask_copy(m):
+    def ask_copy(place):
+        m = member_of(*place)
         return pltpu.make_async_remote_copy(
             src_ref=ask.at[m],
             dst_ref=asked.at[me],
             send_sem=ask_send.at[m],
             recv_sem=ask_recv.at[me],
-            device_id=member_dev(m, z),
+            device_id=dev(*place),
             device_id_type=MESH,
         )
 
     def ask_pair(p, carry):
-        a, b = peer(2 * p, y, z, rep), peer(2 * p + 1, y, z, rep)
+        at_a, at_b = peer(2 * p, y, z, rep), peer(2 * p + 1, y, z, rep)
+        a, b = member_of(*at_a), member_of(*at_b)
         pick_a, pick_b = slots_of(pos, a), slots_of(pos, b)
         picks[a] = pick_a
         picks[b] = pick_b
@@ -331,13 +331,13 @@
 
         @pl.when(p != PAIR_SELF)
         def _():
-            ask_copy(a).start()
+            ask_copy(at_a).start()
 
         @pl.when(p == PAIR_SELF)
         def _():
             asked[me] = ask[me]
 
-        ask_copy(b).start()
+        ask_copy(at_b).start()
         return carry
 
     lax.fori_loop(0, GROUP // 2, ask_pair, 0)
@@ -379,13 +379,14 @@
     def _():
         own.wait()
 
-    def reply_copy(m):
+    def reply_copy(place):
+        m = member_of(*place)
         return pltpu.make_async_remote_copy(
             src_ref=back.at[m],
             dst_ref=replies.at[me],
             send_sem=rep_send.at[m],
             recv_sem=rep_recv.at[me],
-            device_id=member_dev(m, z),
+            device_id=dev(*place),
             device_id_type=MESH,
         )
 
@@ -400,7 +401,8 @@
         ).wait_recv()
 
     def reply_pair(p, carry):
-        a, b = peer_back(2 * p, y, z, rep), peer_back(2 * p + 1, y, z, rep)
+        at_a, at_b = peer_back(2 * p, y, z, rep), peer_back(2 * p + 1, y, z, rep)
+        a, b = member_of(*at_a), member_of(*at_b)
 
         @pl.when(p != PAIR_SELF)
         def _():
@@ -421,13 +423,13 @@
 
         @pl.when(p != PAIR_SELF)
         def _():
-            reply_copy(a).start()
+            reply_copy(at_a).start()
 
         @pl.when(p == PAIR_SELF)
         def _():
             replies[me] = back[me]
 
-        reply_copy(b).start()
+        reply_copy(at_b).start()
         return carry
 
     lax.fori_loop(0, GROUP // 2, reply_pair, 0)
@@ -456,7 +458,8 @@
         ).wait_recv()
 
     def pool_pair(p, carry):
-        a, b = peer(2 * p, y, z, rep), peer(2 * p + 1, y, z, rep)
+        at_a, at_b = peer(2 * p, y, z, rep), peer(2 * p + 1, y, z, rep)
+        a, b = member_of(*at_a), member_of(*at_b)
 
         @pl.when(p != PAIR_SELF)
         def _():
@@ -551,13 +554,14 @@
         copy.start()
         core_copies.append(copy)
 
-    def out_copy(m):
+    def out_copy(place):
+        m = member_of(*place)
         return pltpu.make_async_remote_copy(
             src_ref=out.at[m],
             dst_ref=arrived.at[me],
             send_sem=out_send.at[m],
             recv_sem=out_recv.at[me],
-            device_id=member_dev(m, z),
+            device_id=dev(*place),
             device_id_type=MESH,
         )
 
@@ -571,19 +575,20 @@
         ).astype(bf16)
 
     def pack_pair(p, carry):
-        a, b = peer(2 * p, y, z, rep), peer(2 * p + 1, y, z, rep)
+        at_a, at_b = peer(2 * p, y, z, rep), peer(2 * p + 1, y, z, rep)
+        a, b = member_of(*at_a), member_of(*at_b)
         pack(a)
         pack(b)
 
         @pl.when(p != PAIR_SELF)
         def _():
-            out_copy(a).start()
+            out_copy(at_a).start()
 
         @pl.when(p == PAIR_SELF)
         def _():
             arrived[me] = out[me]
 
-        out_copy(b).start()
+        out_copy(at_b).start()
         return carry
 
     lax.fori_loop(0, 32, pack_pair, 0)
@@ -606,7 +611,8 @@
         ).wait_recv()
 
     def add_pair(p, carry):
-        a, b = peer_back(2 * p, y, z, rep), peer_back(2 * p + 1, y, z, rep)
+        at_a, at_b = peer_back(2 * p, y, z, rep), peer_back(2 * p + 1, y, z, rep)
+        a, b = member_of(*at_a), member_of(*at_b)
 
         @pl.when(p != PAIR_SELF)
         def _():

time: 180 us -> 172 us (0.956)
  Pallas kernels: 172 us -> 164 us
    pallas_call x1, Pallas kernels: 172 us -> 164 us  [step_call(): pl.pallas_call(step_kernel, out_shape=(jax.ShapeDtypeStruct((8, PART, ROW...]
where the time goes in v5:
time: 172 us
  Pallas kernels  164 us (95%)
  other arithmetic  4.11 us (2%)
  local copies, waits for them, and re-layouts  2.96 us (2%)
    pallas_call x1, Pallas kernels, step_call(): pl.pallas_call(step_kernel, out_shape=(jax.ShapeDtypeStruct((8, PART, ROW...  164 us

profile of v5, /device:TPU:2, one launch (start us, length us, event | category | flops | bytes accessed | tf_op | source)
XLA Modules:
  0.0 172.3 jit_solution(14432051576769359262)
XLA Ops:
  0.6 1.3 copy.16
  1.9 0.6 fusion.1.part_ref
  2.6 0.0 copy-start.5
  2.6 0.0 copy-start.2
  2.6 164.4 %shard_map.148 = (f32[8,96,256]{2,1,0:T(8,128)}, f32[32,3456]{1,0:T(8,128)}) custom-call(s32[12,256]{1,0:T(8,128)} %bitcast.25, s32[12,256]{1,0:T(8,128)} %bitcast.26, bf16[96,256]{1,0:T(8,128)(2,1)} %fusion.1.part_ref, bf16[256,128]{1,0:T(8,128)(2,1)} %bottom_ref.1, s32[20,256]{1,0:T(8,128)} %bitcast.24, bf16[20,128,128]{2,1,0:T(8,128)(2,1)} %hot_hbm.1, ...), custom_call_target="tpu_custom_call" | custom-call | tf_op jit(solution)/shard_map/pallas_call | solution.py:920
  167.0 0.0 copy-start.1
  167.0 0.0 copy-start.3
  167.0 1.2 multiply_reduce_fusion
  168.3 0.0 copy-done.5
  168.3 0.0 copy-done.2
  168.3 0.0 copy-done.1
  168.3 0.9 divide_subtract_fusion
  169.2 0.0 copy-done.3
  169.2 0.2 broadcast_multiply_fusion
  169.4 0.3 copy.17
  169.6 0.0 copy-start
  169.7 0.1 reduce_sum.18
  169.7 0.0 copy-start.4
  169.8 0.7 copy-done.4
  170.5 0.6 sqrt_add_fusion
  171.1 0.0 copy-done
  171.1 1.2 fusion
  (3 shorter events, 0.0 us)
Async XLA Ops:
  2.6 165.7 %copy-start.5 = (f32[32]{0:T(128)S(1)}, f32[32]{0:T(128)}, u32[]{:S(2)}) copy-start(f32[32]{0:T(128)} %param.22) | copy-start | bytes 388
  2.6 165.7 %copy-start.2 = (f32[32,3456]{1,0:T(8,128)S(1)}, f32[32,3456]{1,0:T(8,128)}, u32[]{:S(2)}) copy-start(f32[32,3456]{1,0:T(8,128)} %v_wide.1) | copy-start | bytes 1327108
  167.0 1.3 copy-start.1
  167.0 2.2 %copy-start.3 = (f32[8,96,256]{2,1,0:T(8,128)S(1)}, f32[8,96,256]{2,1,0:T(8,128)}, u32[]{:S(2)}) copy-start(f32[8,96,256]{2,1,0:T(8,128)} %get-tuple-element.5) | copy-start | bytes 2359300
  169.6 1.5 copy-start
  169.7 0.8 copy-start.4

commit v6 on v5

--- a/solution.py
+++ b/solution.py
@@ -17,7 +17,7 @@
 GROUP = 64
 ITSELF = 8
 PAIR_SELF = ITSELF // 2
-V_START = 24
+V_START = 16
 WIDE = NCOLD * E
 PART = WIDE // 8
 CROSS = 3456
@@ -126,7 +126,7 @@
     owner_ref, row_ref, part_ref, bottom_ref, ids_ref, hot_hbm, u_ref, v_wide, bias_ref, head_ref, label_ref,
     grad_ref, total_ref,
     hot_ref, v_ref, held, replies, back, ask, asked, pos, tab, rows, picks, pooled,
-    u_full, v_full, first, mixed, low_t, dlow, dpool, grads,
+    u_full, v_full, first, mixed, low_kept, dlow, dpool, grads,
     arrived, out, acc, part_out, part_in, whole,
     core_in, pair, y_in, band, x_in, mine, z_in, strip, summed,
     held_send, held_recv, ask_send, ask_recv, rep_send, rep_recv, own_sem,
@@ -351,12 +351,6 @@
         at = E + WIDE + j * E
         first[:, at : at + E] = jnp.dot(one, hot_ref[j], preferred_element_type=f32).astype(bf16)
 
-    for k in (1, 3, 2):
-        came = ((x + 4 - k) & 3) * 2 + c
-        x_weights(k, came, came, lambda copy: copy.wait_recv())
-        for n in (2, 1, 3):
-            y_weights(k, n, y, (y + n) & 3, lambda copy: copy.start())
-
     def await_part(j, carry):
         sz, srep = source(j)
 
@@ -379,6 +373,12 @@
     def _():
         own.wait()
 
+    for k in (1, 3, 2):
+        came = ((x + 4 - k) & 3) * 2 + c
+        x_weights(k, came, came, lambda copy: copy.wait_recv())
+        for n in (2, 1, 3):
+            y_weights(k, n, y, (y + n) & 3, lambda copy: copy.start())
+
     def reply_copy(place):
         m = member_of(*place)
         return pltpu.make_async_remote_copy(
@@ -433,6 +433,39 @@
         return carry
 
     lax.fori_loop(0, GROUP // 2, reply_pair, 0)
+
+    pooled[...] = jnp.zeros((WIDE, B), f32)
+
+    def await_reply(m):
+        pltpu.make_async_remote_copy(
+            src_ref=back.at[m],
+            dst_ref=replies.at[m],
+            send_sem=rep_send.at[m],
+            recv_sem=rep_recv.at[m],
+            device_id=member_dev(m, z),
+            device_id_type=MESH,
+        ).wait_recv()
+
+    def pool_pair(p, carry):
+        at_a, at_b = peer(2 * p, y, z, rep), peer(2 * p + 1, y, z, rep)
+        a, b = member_of(*at_a), member_of(*at_b)
+
+        @pl.when(p != PAIR_SELF)
+        def _():
+            await_reply(a)
+
+        await_reply(b)
+        got_a = jnp.dot(replies[a], picks[a], preferred_element_type=f32)
+        got_b = jnp.dot(replies[b], picks[b], preferred_element_type=f32)
+        tab_a, tab_b = tab[pl.ds(a, 1), :], tab[pl.ds(b, 1), :]
+        for t in range(NCOLD):
+            more = jnp.where(tab_a == float(t), got_a, 0.0) + jnp.where(
+                tab_b == float(t), got_b, 0.0
+            )
+            pooled[t * E : (t + 1) * E, :] += more
+        return carry
+
+    lax.fori_loop(0, 14, pool_pair, 0)
 
     wc_copies = []
     for k in (1, 3, 2):
@@ -445,38 +478,7 @@
             copy.start()
         wc_copies += forward
 
-    pooled[...] = jnp.zeros((WIDE, B), f32)
-
-    def await_reply(m):
-        pltpu.make_async_remote_copy(
-            src_ref=back.at[m],
-            dst_ref=replies.at[m],
-            send_sem=rep_send.at[m],
-            recv_sem=rep_recv.at[m],
-            device_id=member_dev(m, z),
-            device_id_type=MESH,
-        ).wait_recv()
-
-    def pool_pair(p, carry):
-        at_a, at_b = peer(2 * p, y, z, rep), peer(2 * p + 1, y, z, rep)
-        a, b = member_of(*at_a), member_of(*at_b)
-
-        @pl.when(p != PAIR_SELF)
-        def _():
-            await_reply(a)
-
-        await_reply(b)
-        got_a = jnp.dot(replies[a], picks[a], preferred_element_type=f32)
-        got_b = jnp.dot(replies[b], picks[b], preferred_element_type=f32)
-        tab_a, tab_b = tab[pl.ds(a, 1), :], tab[pl.ds(b, 1), :]
-        for t in range(NCOLD):
-            more = jnp.where(tab_a == float(t), got_a, 0.0) + jnp.where(
-                tab_b == float(t), got_b, 0.0
-            )
-            pooled[t * E : (t + 1) * E, :] += more
-        return carry
-
-    lax.fori_loop(0, 20, pool_pair, 0)
+    lax.fori_loop(14, 24, pool_pair, 0)
 
     for k in range(4):
         came = ((x + 4 - k) & 3) * 2 + other_c
@@ -489,13 +491,13 @@
     low = jnp.dot(first[:, 0:E], u_full[0:E, :], preferred_element_type=f32)
     low = low + jnp.dot(first[:, hot_at:], u_full[hot_at:, :], preferred_element_type=f32)
 
-    lax.fori_loop(20, 32, pool_pair, 0)
+    lax.fori_loop(24, 32, pool_pair, 0)
     for t in range(NCOLD):
         first[:, E + t * E : E + (t + 1) * E] = pooled[t * E : (t + 1) * E, :].T.astype(bf16)
 
     low = low + jnp.dot(first[:, E:hot_at], u_full[E:hot_at, :], preferred_element_type=f32)
     low_half = low.astype(bf16)
-    low_t[...] = low.T.astype(bf16)
+    low_kept[...] = low_half
 
     def cols(i, width):
         return pl.ds(pl.multiple_of(i * width, width), width)
@@ -521,13 +523,11 @@
     dlogit = jax.nn.sigmoid(logit) - label[:, 0:1]
 
     dlow[...] = jnp.zeros((B, RANK), f32)
-    grads[:, CROSS:] = jnp.zeros((RANK, PADDED - CROSS), bf16)
 
     def backward_cols(i, carry):
         at = cols(i, COLS)
         dmix = (dlogit * line(head_ref, i) * first[:, at].astype(f32)).astype(bf16)
         dlow[...] += lax.dot_general(dmix, v_full[:, at], NT, preferred_element_type=f32)
-        grads[:, at] = jnp.dot(low_t[...], dmix, preferred_element_type=f32).astype(bf16)
         return carry
 
     lax.fori_loop(0, CROSS // COLS, backward_cols, 0)
@@ -537,6 +537,56 @@
         direct = dlogit * head_ref[t + 1 : t + 2, :] * (mixed[:, lo:hi] + 1.0)
         through = lax.dot_general(u_full[lo:hi, :], dlow_half, NT, preferred_element_type=f32)
         dpool[t * E : (t + 1) * E, :] = (direct.T + through).astype(bf16).astype(f32)
+
+    def out_copy(place):
+        m = member_of(*place)
+        return pltpu.make_async_remote_copy(
+            src_ref=out.at[m],
+            dst_ref=arrived.at[me],
+            send_sem=out_send.at[m],
+            recv_sem=out_recv.at[me],
+            device_id=dev(*place),
+            device_id_type=MESH,
+        )
+
+    def pack(m):
+        which = tab[pl.ds(m, 1), :]
+        chosen = dpool[0:E, :]
+        for t in range(1, NCOLD):
+            chosen = jnp.where(which == float(t), dpool[t * E : (t + 1) * E, :], chosen)
+        out[m] = lax.dot_general(
+            chosen.astype(bf16), picks[m], NT, preferred_element_type=f32
+        ).astype(bf16)
+
+    def pack_pair(p, carry):
+        at_a, at_b = peer(2 * p, y, z, rep), peer(2 * p + 1, y, z, rep)
+        a, b = member_of(*at_a), member_of(*at_b)
+        pack(a)
+        pack(b)
+
+        @pl.when(p != PAIR_SELF)
+        def _():
+            out_copy(at_a).start()
+
+        @pl.when(p == PAIR_SELF)
+        def _():
+            arrived[me] = out[me]
+
+        out_copy(at_b).start()
+        return carry
+
+    lax.fori_loop(0, 32, pack_pair, 0)
+
+    grads[:, CROSS:] = jnp.zeros((RANK, PADDED - CROSS), bf16)
+    low_t = low_kept[...].astype(f32).T.astype(bf16)
+
+    def grad_cols(i, carry):
+        at = cols(i, COLS)
+        dmix = (dlogit * line(head_ref, i) * first[:, at].astype(f32)).astype(bf16)
+        grads[:, at] = jnp.dot(low_t, dmix, preferred_element_type=f32).astype(bf16)
+        return carry
+
+    lax.fori_loop(0, CROSS // COLS, grad_cols, 0)
 
     def v_rows(r):
         return pl.ds(pl.multiple_of(r * V_ROWS, V_ROWS), V_ROWS)
@@ -554,50 +604,6 @@
         copy.start()
         core_copies.append(copy)
 
-    def out_copy(place):
-        m = member_of(*place)
-        return pltpu.make_async_remote_copy(
-            src_ref=out.at[m],
-            dst_ref=arrived.at[me],
-            send_sem=out_send.at[m],
-            recv_sem=out_recv.at[me],
-            device_id=dev(*place),
-            device_id_type=MESH,
-        )
-
-    def pack(m):
-        which = tab[pl.ds(m, 1), :]
-        chosen = dpool[0:E, :]
-        for t in range(1, NCOLD):
-            chosen = jnp.where(which == float(t), dpool[t * E : (t + 1) * E, :], chosen)
-        out[m] = lax.dot_general(
-            chosen.astype(bf16), picks[m], NT, preferred_element_type=f32
-        ).astype(bf16)
-
-    def pack_pair(p, carry):
-        at_a, at_b = peer(2 * p, y, z, rep), peer(2 * p + 1, y, z, rep)
-        a, b = member_of(*at_a), member_of(*at_b)
-        pack(a)
-        pack(b)
-
-        @pl.when(p != PAIR_SELF)
-        def _():
-            out_copy(at_a).start()
-
-        @pl.when(p == PAIR_SELF)
-        def _():
-            arrived[me] = out[me]
-
-        out_copy(at_b).start()
-        return carry
-
-    lax.fori_loop(0, 32, pack_pair, 0)
-
-    for k in range(4):
-        core_copies[k].wait_recv()
-        pair[k] = (grads[v_rows(2 * k + c), :].astype(f32) + core_in[k].astype(f32)).astype(bf16)
-
-
     acc[...] = jnp.zeros((WIDE, ROWS), f32)
 
     def await_out(m):
@@ -629,6 +635,11 @@
         return carry
 
     lax.fori_loop(0, V_START, add_pair, 0)
+
+    for k in range(4):
+        core_copies[k].wait_recv()
+        pair[k] = (grads[v_rows(2 * k + c), :].astype(f32) + core_in[k].astype(f32)).astype(bf16)
+
 
     def piece(j):
         return pl.ds(pl.multiple_of(j * V_PIECE, V_PIECE), V_PIECE)
@@ -725,6 +736,44 @@
         return carry
 
     lax.fori_loop(1, 16, z_start, 0)
+
+    def await_sum(j, carry):
+        sz, srep = holder(j)
+
+        @pl.when(is_other((sz, srep)))
+        def _():
+            pltpu.make_async_remote_copy(
+                src_ref=part_out.at[0],
+                dst_ref=part_in.at[sz >> 1],
+                send_sem=part_send.at[0],
+                recv_sem=part_recv.at[sz >> 1],
+                device_id=dev(y, sz, srep),
+                device_id_type=MESH,
+            ).wait_recv()
+
+        return carry
+
+    lax.fori_loop(0, 8, await_sum, 0)
+    total = part_in[0].astype(f32)
+    for g in range(1, 8):
+        total = total + part_in[g].astype(f32)
+    whole[rep] = total.astype(bf16)
+
+    def all_copy(j):
+        return pltpu.make_async_remote_copy(
+            src_ref=whole.at[rep],
+            dst_ref=whole.at[rep],
+            send_sem=all_send.at[j],
+            recv_sem=all_recv.at[rep],
+            device_id=dev(y, z, (rep + j) & 7),
+            device_id_type=MESH,
+        )
+
+    def send_all(j, carry):
+        all_copy(j).start()
+        return carry
+
+    lax.fori_loop(1, 8, send_all, 0)
 
     def zb_copy(k):
         return pltpu.make_async_remote_copy(
@@ -768,44 +817,6 @@
         out_copy(m).wait_send()
 
     others(GROUP, drain)
-
-    def await_sum(j, carry):
-        sz, srep = holder(j)
-
-        @pl.when(is_other((sz, srep)))
-        def _():
-            pltpu.make_async_remote_copy(
-                src_ref=part_out.at[0],
-                dst_ref=part_in.at[sz >> 1],
-                send_sem=part_send.at[0],
-                recv_sem=part_recv.at[sz >> 1],
-                device_id=dev(y, sz, srep),
-                device_id_type=MESH,
-            ).wait_recv()
-
-        return carry
-
-    lax.fori_loop(0, 8, await_sum, 0)
-    total = part_in[0].astype(f32)
-    for g in range(1, 8):
-        total = total + part_in[g].astype(f32)
-    whole[rep] = total.astype(bf16)
-
-    def all_copy(j):
-        return pltpu.make_async_remote_copy(
-            src_ref=whole.at[rep],
-            dst_ref=whole.at[rep],
-            send_sem=all_send.at[j],
-            recv_sem=all_recv.at[rep],
-            device_id=dev(y, z, (rep + j) & 7),
-            device_id_type=MESH,
-        )
-
-    def send_all(j, carry):
-        all_copy(j).start()
-        return carry
-
-    lax.fori_loop(1, 8, send_all, 0)
 
     def zb_wait(k, carry):
         other = (z + 16 - k) & 15
@@ -944,7 +955,7 @@
             pltpu.VMEM((RANK, CROSS), bf16),
             pltpu.VMEM((B, CROSS), bf16),
             pltpu.VMEM((B, CROSS), f32),
-            pltpu.VMEM((RANK, B), bf16),
+            pltpu.VMEM((B, RANK), bf16),
             pltpu.VMEM((B, RANK), f32),
             pltpu.VMEM((WIDE, B), f32),
             pltpu.VMEM((RANK, PADDED), bf16),

time: 172 us -> 177 us (1.029)
  the two profiles are of different devices: /device:TPU:2 before, /device:TPU:12 now
where the time goes in v6:
time: 177 us
  Pallas kernels  169 us (95%)
  other arithmetic  4.11 us (2%)
  local copies, waits for them, and re-layouts  2.96 us (2%)
    pallas_call x1, Pallas kernels, step_call(): pl.pallas_call(step_kernel, out_shape=(jax.ShapeDtypeStruct((8, PART, ROW...  169 us

profile of v6, /device:TPU:12, one launch (start us, length us, event | category | flops | bytes accessed | tf_op | source)
XLA Modules:
  0.0 177.0 jit_solution(3645232344671439802)
XLA Ops:
  0.6 1.3 copy.16
  1.9 0.6 fusion.1.part_ref
  2.6 0.0 copy-start.5
  2.6 0.0 copy-start.2
  2.6 169.2 %shard_map.148 = (f32[8,96,256]{2,1,0:T(8,128)}, f32[32,3456]{1,0:T(8,128)}) custom-call(s32[12,256]{1,0:T(8,128)} %bitcast.25, s32[12,256]{1,0:T(8,128)} %bitcast.26, bf16[96,256]{1,0:T(8,128)(2,1)} %fusion.1.part_ref, bf16[256,128]{1,0:T(8,128)(2,1)} %bottom_ref.1, s32[20,256]{1,0:T(8,128)} %bitcast.24, bf16[20,128,128]{2,1,0:T(8,128)(2,1)} %hot_hbm.1, ...), custom_call_target="tpu_custom_call" | custom-call | tf_op jit(solution)/shard_map/pallas_call | solution.py:931
  171.8 0.0 copy-start.1
  171.8 0.0 copy-start.3
  171.8 1.2 multiply_reduce_fusion
  173.1 0.0 copy-done.5
  173.1 0.0 copy-done.2
  173.1 0.0 copy-done.1
  173.1 0.9 divide_subtract_fusion
  174.0 0.0 copy-done.3
  174.0 0.2 broadcast_multiply_fusion
  174.2 0.3 copy.17
  174.4 0.0 copy-start
  174.4 0.1 reduce_sum.18
  174.5 0.0 copy-start.4
  174.5 0.7 copy-done.4
  175.3 0.6 sqrt_add_fusion
  175.9 0.0 copy-done
  175.9 1.2 fusion
  (3 shorter events, 0.0 us)
Async XLA Ops:
  2.6 170.5 %copy-start.5 = (f32[32]{0:T(128)S(1)}, f32[32]{0:T(128)}, u32[]{:S(2)}) copy-start(f32[32]{0:T(128)} %param.22) | copy-start | bytes 388
  2.6 170.5 %copy-start.2 = (f32[32,3456]{1,0:T(8,128)S(1)}, f32[32,3456]{1,0:T(8,128)}, u32[]{:S(2)}) copy-start(f32[32,3456]{1,0:T(8,128)} %v_wide.1) | copy-start | bytes 1327108
  171.8 1.3 copy-start.1
  171.8 2.2 %copy-start.3 = (f32[8,96,256]{2,1,0:T(8,128)S(1)}, f32[8,96,256]{2,1,0:T(8,128)}, u32[]{:S(2)}) copy-start(f32[8,96,256]{2,1,0:T(8,128)} %get-tuple-element.5) | copy-start | bytes 2359300
  174.4 1.5 copy-start
  174.5 0.8 copy-start.4
